TPU v7x, 32 devices: a whole 2x2x4 slice. The times are simulated.
32 devices in a mesh: ctx: 16 (over z, y, x), tp: 2 (over core).
Axes of the slice: x: 2, y: 2, z: 4, core: 2. Of those that a mesh axis runs over, the one named last changes fastest.
Arguments:
- tokens: bfloat16 [4096, 896], P('ctx'), may hold values from -6 to 6
- attn_gain: bfloat16 [896], replicated, may hold values from 0.5 to 1.5
- w_query: bfloat16 [896, 896], P(None, 'tp'), may hold values from -0.1875 to 0.1875
- b_query: bfloat16 [896], P('tp'), may hold values from -3 to 3
- w_key: bfloat16 [896, 128], P(None, 'tp'), may hold values from -0.1875 to 0.1875
- b_key: bfloat16 [128], P('tp'), may hold values from -3 to 3
- w_value: bfloat16 [896, 128], P(None, 'tp'), may hold values from -0.1875 to 0.1875
- b_value: bfloat16 [128], P('tp'), may hold values from -3 to 3
- w_out: bfloat16 [896, 896], P('tp'), may hold values from -3 to 3
- mlp_gain: bfloat16 [896], replicated, may hold values from 0.5 to 1.5
- w_gate: bfloat16 [896, 4864], P(None, 'tp'), may hold values from -0.1875 to 0.1875
- w_up: bfloat16 [896, 4864], P(None, 'tp'), may hold values from -0.1875 to 0.1875
- w_down: bfloat16 [4864, 896], P('tp'), may hold values from -0.15625 to 0.15625
- cotangent: bfloat16 [4096, 896], P('ctx'), may hold values from -6 to 6
- block_table: int32 [16], replicated, may hold values from 0 to 15, each once
- doc_lengths: int32 [2, 6], replicated, may hold values from 1 to 1536, as said below
Outputs:
- mixed: bfloat16 [4096, 896], P('ctx')
- grad_tokens: float32 [4096, 896], P('ctx')
- grad_attn_gain: float32 [896], replicated
- grad_w_query: float32 [896, 896], P('ctx', 'tp')
- grad_b_query: float32 [896], P('tp')
- grad_w_key: float32 [896, 128], P('ctx', 'tp')
- grad_b_key: float32 [128], P('tp')
- grad_w_value: float32 [896, 128], P('ctx', 'tp')
- grad_b_value: float32 [128], P('tp')
- grad_w_out: float32 [896, 896], P('tp', 'ctx')
- grad_mlp_gain: float32 [896], replicated
- grad_w_gate: float32 [896, 4864], P('ctx', 'tp')
- grad_w_up: float32 [896, 4864], P('ctx', 'tp')
- grad_w_down: float32 [4864, 896], P('tp', 'ctx')
Inputs may be any that keep to these rules, and one draw needn't show every extreme that they name: A permutation: index c of ctx holds blocks block_table[c] and 31 - block_table[c] of every sequence. `doc_lengths`: each row sums to 2048; the first document of every sequence holds at least half of its tokens and is its longest.
All inputs are finite; a program needn't handle non-finite values.
Results may differ from a plain program's by a relative error of at most 0.04.
Values may be sent and summed in bfloat16 or wider, within the bound.
A program may use at most 192 MiB of HBM per device.

v0:
```python
import functools

import jax
import jax.numpy as jnp
from jax import lax
from jax.experimental import pallas as pl
from jax.experimental.pallas import tpu as pltpu
from jax.sharding import PartitionSpec as P

EPSILON = 1e-06
THETA = 1000000.0
NEGATIVE = -1e30
KEY_BLOCK = 256
VMEM_BYTES = 40 * 1024 * 1024
CONTRACT_LAST = (((1,), (1,)), ((), ()))
CONTRACT_FIRST = (((0,), (0,)), ((), ()))


def rope_tables(positions, head_width):
    half_width = head_width // 2
    frequency = THETA ** (-jnp.arange(half_width, dtype=jnp.float32) * 2.0 / head_width)
    angles = positions.astype(jnp.float32)[:, None] * frequency[None, :]
    return (jnp.cos(angles), jnp.sin(angles))


def rotate(values, cos_table, sin_table):
    half_width = values.shape[-1] // 2
    cos_part = cos_table[:, None, :]
    sin_part = sin_table[:, None, :]
    first_half = values[..., :half_width]
    second_half = values[..., half_width:]
    return jnp.concatenate(
        [
            first_half * cos_part - second_half * sin_part,
            second_half * cos_part + first_half * sin_part,
        ],
        axis=-1,
    )


def norm_back(grad_normed, inputs, inverse, gain_f):
    scaled = grad_normed * gain_f
    grad_in = inverse * scaled - inputs * (inverse * inverse * inverse) * jnp.mean(
        scaled * inputs, axis=1, keepdims=True
    )
    grad_gain = jnp.sum(grad_normed * inputs * inverse, axis=0)
    return (grad_in, grad_gain)


def swap(values, axis_name, bit):
    size = lax.axis_size(axis_name)
    return lax.ppermute(values, axis_name, [(i, i ^ bit) for i in range(size)])


def sum_pair(part):
    low = part.astype(jnp.bfloat16)
    return low.astype(jnp.float32) + swap(low, "tp", 1).astype(jnp.float32)


def bit_list(count):
    return [1 << b for b in range(count.bit_length() - 1)]


def scatter_rows(matrix, order):
    index = lax.axis_index("ctx")
    count = lax.axis_size("ctx")
    rows, columns = matrix.shape
    block = rows // count
    cur = matrix
    left = sorted(order, reverse=True)
    for bit in order:
        at = left.index(bit)
        before = 1 << at
        after = 1 << (len(left) - at - 1)
        shaped = cur.reshape(before, 2, after * block, columns)
        mine = (index // bit) % 2
        keep = lax.dynamic_index_in_dim(shaped, mine, 1, keepdims=False)
        send = lax.dynamic_index_in_dim(shaped, 1 - mine, 1, keepdims=False)
        got = swap(send, "ctx", bit)
        total = keep.astype(jnp.float32) + got.astype(jnp.float32)
        left.remove(bit)
        if left:
            cur = total.astype(jnp.bfloat16).reshape(before * after * block, columns)
        else:
            cur = total.reshape(block, columns)
    return cur


def stack_heads(rows, head_dim):
    heads = rows.shape[1] // head_dim
    return jnp.concatenate(
        [rows[:, h * head_dim : (h + 1) * head_dim] for h in range(heads)], axis=0
    )


def unstack_heads(stacked, count):
    heads = stacked.shape[0] // count
    return jnp.concatenate([stacked[h * count : (h + 1) * count] for h in range(heads)], axis=1)


def sort_blocks(slot_ref, kv_ref, sorted_ref):
    blocks, block_len = kv_ref.shape[1], kv_ref.shape[2]

    def move(b, carry):
        sorted_ref[pl.ds(pl.multiple_of(b * block_len, block_len), block_len), :] = kv_ref[
            0, slot_ref[b]
        ]
        return carry

    lax.fori_loop(0, blocks, move, 0)


def forward_kernel(
    key_len, slot_ref, low_ref, high_ref, q_ref, kv_ref, pos_ref, first_ref,
    attn_ref, low_attn_ref, log_ref, sorted_ref,
):
    step = pl.program_id(0) * pl.num_programs(1) + pl.program_id(1)
    head_dim = kv_ref.shape[3] // 2
    count = q_ref.shape[0]

    @pl.when(pl.program_id(1) == 0)
    def _():
        sort_blocks(slot_ref, kv_ref, sorted_ref)

    queries = stack_heads(q_ref[...].astype(jnp.float32), head_dim).astype(jnp.bfloat16)
    rows = queries.shape[0]
    q_pos, q_first = pos_ref[0], first_ref[0]

    def body(j, carry):
        top, total, acc = carry
        start = pl.multiple_of(j * key_len, key_len)
        both = sorted_ref[pl.ds(start, key_len), :]
        keys, values = both[:, :head_dim], both[:, head_dim:]
        scores = lax.dot_general(keys, queries, CONTRACT_LAST, preferred_element_type=jnp.float32)
        k_pos = start + lax.broadcasted_iota(jnp.int32, scores.shape, 0)
        seen = (k_pos <= q_pos) & (k_pos >= q_first)
        scores = jnp.where(seen, scores, NEGATIVE)
        new_top = jnp.maximum(top, jnp.max(scores, axis=0, keepdims=True))
        weights = jnp.where(seen, jnp.exp(scores - new_top), 0.0)
        factor = jnp.exp(top - new_top)
        total = total * factor + jnp.sum(weights, axis=0, keepdims=True)
        acc = acc * factor + lax.dot_general(
            values, weights.astype(jnp.bfloat16), CONTRACT_FIRST,
            preferred_element_type=jnp.float32,
        )
        return new_top, total, acc

    init = (
        jnp.full((1, rows), NEGATIVE, jnp.float32),
        jnp.zeros((1, rows), jnp.float32),
        jnp.zeros((head_dim, rows), jnp.float32),
    )
    top, total, acc = lax.fori_loop(low_ref[step], high_ref[step], body, init)
    out = unstack_heads((acc / total).T, count)
    attn_ref[...] = out
    low_attn_ref[...] = out.astype(jnp.bfloat16)
    log_ref[0] = top + jnp.log(total)


def backward_kernel(
    key_len, scale, slot_ref, low_ref, high_ref, block_ref, q_ref, kv_ref, pos_ref, first_ref,
    attn_ref, log_ref, grad_ref, grad_q_ref, grad_kv_ref, sorted_ref, acc_ref,
):
    step = pl.program_id(0) * pl.num_programs(1) + pl.program_id(1)
    head_dim = kv_ref.shape[3] // 2
    blocks, block_len = kv_ref.shape[1], kv_ref.shape[2]
    count = q_ref.shape[0]

    @pl.when(pl.program_id(1) == 0)
    def _():
        sort_blocks(slot_ref, kv_ref, sorted_ref)
        acc_ref[...] = jnp.zeros_like(acc_ref)

    queries = stack_heads(q_ref[...].astype(jnp.float32), head_dim).astype(jnp.bfloat16)
    grad_f = grad_ref[...].astype(jnp.float32)
    grads = stack_heads(grad_f, head_dim).astype(jnp.bfloat16)
    delta = jnp.sum(stack_heads(grad_f * attn_ref[...], head_dim).T, axis=0, keepdims=True)
    rows = queries.shape[0]
    q_pos, q_first, log_total = pos_ref[0], first_ref[0], log_ref[0]

    def body(j, grad_q):
        start = pl.multiple_of(j * key_len, key_len)
        both = sorted_ref[pl.ds(start, key_len), :]
        keys, values = both[:, :head_dim], both[:, head_dim:]
        scores = lax.dot_general(keys, queries, CONTRACT_LAST, preferred_element_type=jnp.float32)
        k_pos = start + lax.broadcasted_iota(jnp.int32, scores.shape, 0)
        seen = (k_pos <= q_pos) & (k_pos >= q_first)
        shares = jnp.where(seen, jnp.exp(jnp.where(seen, scores - log_total, 0.0)), 0.0)
        grad_shares = lax.dot_general(
            values, grads, CONTRACT_LAST, preferred_element_type=jnp.float32
        )
        grad_scores = (shares * (grad_shares - delta)).astype(jnp.bfloat16)
        grad_values = jnp.dot(
            shares.astype(jnp.bfloat16), grads, preferred_element_type=jnp.float32
        )
        grad_keys = jnp.dot(grad_scores, queries, preferred_element_type=jnp.float32)
        acc_ref[pl.ds(start, key_len), :] += jnp.concatenate([grad_keys, grad_values], axis=1)
        return grad_q + lax.dot_general(
            keys, grad_scores, CONTRACT_FIRST, preferred_element_type=jnp.float32
        )

    grad_q = lax.fori_loop(
        low_ref[step], high_ref[step], body, jnp.zeros((head_dim, rows), jnp.float32)
    )
    grad_q_ref[...] = unstack_heads(grad_q.T, count) * scale

    @pl.when(pl.program_id(1) == pl.num_programs(1) - 1)
    def _():
        def move(k, carry):
            at = pl.multiple_of(block_ref[k] * block_len, block_len)
            grad_kv_ref[0, k] = acc_ref[pl.ds(at, block_len), :].astype(jnp.bfloat16)
            return carry

        lax.fori_loop(0, blocks, move, 0)


def attention(seq_count, key_len, head_dim, plan, queries, key_values, pos, first):
    rows, width = queries.shape
    blocks, block_len = key_values.shape[1:3]
    stacked = pos.shape[2]
    row_spec = pl.BlockSpec((block_len, width), lambda s, j, *_: (s * 2 + j, 0))
    kv_spec = pl.BlockSpec((1, blocks, block_len, 2 * head_dim), lambda s, j, *_: (s, 0, 0, 0))
    lane_spec = pl.BlockSpec((1, 1, stacked), lambda s, j, *_: (s * 2 + j, 0, 0))
    flops = 2 * 2 * rows * width * blocks * block_len // 2
    sorted_shape = pltpu.VMEM((blocks * block_len, 2 * head_dim), jnp.bfloat16)
    params = pltpu.CompilerParams(vmem_limit_bytes=VMEM_BYTES)

    def forward():
        return pl.pallas_call(
            functools.partial(forward_kernel, key_len),
            grid_spec=pltpu.PrefetchScalarGridSpec(
                num_scalar_prefetch=3,
                grid=(seq_count, 2),
                in_specs=[row_spec, kv_spec, lane_spec, lane_spec],
                out_specs=[row_spec, row_spec, lane_spec],
                scratch_shapes=[sorted_shape],
            ),
            out_shape=[
                jax.ShapeDtypeStruct((rows, width), jnp.float32),
                jax.ShapeDtypeStruct((rows, width), jnp.bfloat16),
                jax.ShapeDtypeStruct(pos.shape, jnp.float32),
            ],
            compiler_params=params,
            cost_estimate=pl.CostEstimate(
                flops=flops * 2, bytes_accessed=4000000, transcendentals=flops // 128
            ),
        )(*plan[:3], queries, key_values, pos, first)

    def backward(attended, log_total, grads):
        return pl.pallas_call(
            functools.partial(backward_kernel, key_len, head_dim ** (-0.5)),
            grid_spec=pltpu.PrefetchScalarGridSpec(
                num_scalar_prefetch=4,
                grid=(seq_count, 2),
                in_specs=[row_spec, kv_spec, lane_spec, lane_spec, row_spec, lane_spec, row_spec],
                out_specs=[row_spec, kv_spec],
                scratch_shapes=[
                    sorted_shape,
                    pltpu.VMEM((blocks * block_len, 2 * head_dim), jnp.float32),
                ],
            ),
            out_shape=[
                jax.ShapeDtypeStruct((rows, width), jnp.float32),
                jax.ShapeDtypeStruct(key_values.shape, jnp.bfloat16),
            ],
            compiler_params=params,
            cost_estimate=pl.CostEstimate(
                flops=flops * 5, bytes_accessed=8000000, transcendentals=flops // 128
            ),
        )(*plan, queries, key_values, pos, first, attended, log_total, grads)

    return forward, backward


def shards(
    tokens,
    attn_gain,
    w_query,
    b_query,
    w_key,
    b_key,
    w_value,
    b_value,
    w_out,
    mlp_gain,
    w_gate,
    w_up,
    w_down,
    cotangent,
    block_table,
    doc_lengths,
):
    tok_rows, model_width = tokens.shape
    head_dim = w_key.shape[1]
    group = w_query.shape[1] // head_dim
    seq_count = doc_lengths.shape[0]
    half_rows = tok_rows // seq_count
    block_len = half_rows // 2
    ctx_size = lax.axis_size("ctx")
    seq_len = ctx_size * half_rows
    scale = head_dim ** (-0.5)
    own_index = lax.axis_index("ctx")
    pair_blocks = jnp.stack([block_table, 2 * ctx_size - 1 - block_table], axis=1)
    all_pos = (
        pair_blocks[:, :, None] * block_len + jnp.arange(block_len, dtype=jnp.int32)[None, None, :]
    ).reshape(seq_len)
    own_pos = lax.dynamic_slice_in_dim(all_pos, own_index * half_rows, half_rows)
    bits = bit_list(ctx_size)
    masks = [0]
    for bit in reversed(bits):
        masks = masks + [m ^ bit for m in masks]
    slots = jnp.array(masks, jnp.int32) ^ own_index
    key_blocks = pair_blocks[slots].reshape(2 * ctx_size)
    block_ids = jnp.arange(2 * ctx_size, dtype=jnp.int32)
    block_slots = jnp.sum(
        jnp.where(key_blocks[None, :] == block_ids[:, None], block_ids[None, :], 0), axis=1
    ).astype(jnp.int32)
    bounds = jnp.cumsum(doc_lengths, axis=1)
    own_first = jnp.max(
        jnp.where(own_pos[None, :, None] >= bounds[:, None, :], bounds[:, None, :], 0), axis=2
    )
    cos_table, sin_table = rope_tables(own_pos, head_dim)
    key_len = min(KEY_BLOCK, seq_len)
    pos_blocks = jnp.broadcast_to(
        own_pos.reshape(1, 2, block_len), (seq_count, 2, block_len)
    ).reshape(2 * seq_count, block_len)
    first_blocks = own_first.reshape(2 * seq_count, block_len)
    plan = (
        block_slots,
        first_blocks[:, 0] // key_len,
        pos_blocks[:, -1] // key_len + 1,
        key_blocks,
    )
    lane_pos = jnp.tile(pos_blocks, (1, group))[:, None, :]
    lane_first = jnp.tile(first_blocks, (1, group))[:, None, :]
    x_float = tokens.astype(jnp.float32)
    gain_one = attn_gain.astype(jnp.float32)
    gain_two = mlp_gain.astype(jnp.float32)
    inv_one = lax.rsqrt(jnp.mean(x_float * x_float, axis=1, keepdims=True) + EPSILON)
    normed = (x_float * inv_one * gain_one).astype(jnp.bfloat16)
    query_pre = jnp.dot(normed, w_query, preferred_element_type=jnp.float32) + b_query.astype(
        jnp.float32
    )
    key_pre = jnp.dot(normed, w_key, preferred_element_type=jnp.float32) + b_key.astype(jnp.float32)
    value_rows = (
        jnp.dot(normed, w_value, preferred_element_type=jnp.float32) + b_value.astype(jnp.float32)
    ).astype(jnp.bfloat16)
    query_rot = rotate(
        query_pre.reshape(seq_count, half_rows, group, head_dim), cos_table, sin_table
    ).astype(jnp.bfloat16)
    query_low = (query_rot.astype(jnp.float32) * scale).astype(jnp.bfloat16).reshape(tok_rows, group * head_dim)
    key_local = (
        rotate(key_pre.reshape(seq_count, half_rows, 1, head_dim), cos_table, sin_table)
        .reshape(seq_count, half_rows, head_dim)
        .astype(jnp.bfloat16)
    )
    value_local = value_rows.reshape(seq_count, half_rows, head_dim)

    gathered = jnp.concatenate([key_local, value_local], axis=2)
    for bit in reversed(bits):
        gathered = jnp.concatenate([gathered, swap(gathered, "ctx", bit)], axis=1)
    key_values = gathered.reshape(seq_count, 2 * ctx_size, block_len, 2 * head_dim)
    attend, attend_back = attention(
        seq_count, key_len, head_dim, plan, query_low, key_values, lane_pos, lane_first
    )
    attended, attn_low, log_total = attend()
    branch = sum_pair(jnp.dot(attn_low, w_out, preferred_element_type=jnp.float32))
    stream = x_float + branch
    inv_two = lax.rsqrt(jnp.mean(stream * stream, axis=1, keepdims=True) + EPSILON)
    normed_two = (stream * inv_two * gain_two).astype(jnp.bfloat16)
    gate_pre = jnp.dot(normed_two, w_gate, preferred_element_type=jnp.float32)
    upward = jnp.dot(normed_two, w_up, preferred_element_type=jnp.float32)
    sigmoid_gate = jax.nn.sigmoid(gate_pre)
    swish = gate_pre * sigmoid_gate
    hidden = (swish * upward).astype(jnp.bfloat16)
    down_part = sum_pair(jnp.dot(hidden, w_down, preferred_element_type=jnp.float32))
    mixed = (stream + down_part).astype(jnp.bfloat16)
    grad_f = cotangent.astype(jnp.float32)
    grad_w_down = jnp.dot(cotangent.T, hidden, preferred_element_type=jnp.float32)
    grad_hidden = jnp.dot(cotangent, w_down.T, preferred_element_type=jnp.float32)
    grad_gate_low = (
        grad_hidden * upward * sigmoid_gate * (1.0 + gate_pre * (1.0 - sigmoid_gate))
    ).astype(jnp.bfloat16)
    grad_up_low = (grad_hidden * swish).astype(jnp.bfloat16)
    grad_w_gate = jnp.dot(normed_two.T, grad_gate_low, preferred_element_type=jnp.float32)
    grad_w_up = jnp.dot(normed_two.T, grad_up_low, preferred_element_type=jnp.float32)
    grad_normed_part = jnp.dot(
        grad_gate_low, w_gate.T, preferred_element_type=jnp.float32
    ) + jnp.dot(grad_up_low, w_up.T, preferred_element_type=jnp.float32)
    grad_normed_two = sum_pair(grad_normed_part)
    grad_stream_part, grad_mlp_gain = norm_back(grad_normed_two, stream, inv_two, gain_two)
    grad_stream = grad_f + grad_stream_part
    grad_branch = grad_stream.astype(jnp.bfloat16)
    grad_w_out = jnp.dot(grad_branch.T, attn_low, preferred_element_type=jnp.float32)
    grad_attn_low = jnp.dot(grad_branch, w_out.T, preferred_element_type=jnp.float32).astype(
        jnp.bfloat16
    )
    grad_query_rows, grad_key_values = attend_back(attended, log_total, grad_attn_low)
    cur = grad_key_values.reshape(seq_count, seq_len, 2 * head_dim)
    for bit in bits:
        half = cur.shape[1] // 2
        total = cur[:, :half].astype(jnp.float32) + swap(cur[:, half:], "ctx", bit).astype(
            jnp.float32
        )
        cur = total if bit == bits[-1] else total.astype(jnp.bfloat16)
    grad_keys_own = cur[:, :, :head_dim]
    grad_values_own = cur[:, :, head_dim:]
    grad_query_rows = grad_query_rows.reshape(seq_count, half_rows, group, head_dim)
    grad_query_low = (
        rotate(grad_query_rows, cos_table, -sin_table)
        .reshape(tok_rows, group * head_dim)
        .astype(jnp.bfloat16)
    )
    grad_key_low = (
        rotate(grad_keys_own.reshape(seq_count, half_rows, 1, head_dim), cos_table, -sin_table)
        .reshape(tok_rows, head_dim)
        .astype(jnp.bfloat16)
    )
    grad_value_low = grad_values_own.reshape(tok_rows, head_dim).astype(jnp.bfloat16)
    grad_w_query = jnp.dot(normed.T, grad_query_low, preferred_element_type=jnp.float32)
    grad_w_key = jnp.dot(normed.T, grad_key_low, preferred_element_type=jnp.float32)
    grad_w_value = jnp.dot(normed.T, grad_value_low, preferred_element_type=jnp.float32)
    grad_b_query = jnp.sum(grad_query_low.astype(jnp.float32), axis=0)
    grad_b_key = jnp.sum(grad_key_low.astype(jnp.float32), axis=0)
    grad_b_value = jnp.sum(grad_value_low.astype(jnp.float32), axis=0)
    grad_first_part = (
        jnp.dot(grad_query_low, w_query.T, preferred_element_type=jnp.float32)
        + jnp.dot(grad_key_low, w_key.T, preferred_element_type=jnp.float32)
        + jnp.dot(grad_value_low, w_value.T, preferred_element_type=jnp.float32)
    )
    grad_normed = sum_pair(grad_first_part)
    grad_in_part, grad_attn_gain = norm_back(grad_normed, x_float, inv_one, gain_one)
    grad_tokens = grad_stream + grad_in_part
    other = [bits[1], bits[0]] + bits[2:]

    def scatter(matrix, order):
        return scatter_rows(matrix.astype(jnp.bfloat16), order)

    last = bits[2:] + bits[:2]
    sum_down = scatter(grad_w_down, last).T
    sum_gate = scatter(grad_w_gate, bits)
    sum_up = scatter(grad_w_up, other)
    sum_out = scatter(grad_w_out, other).T
    sum_query = scatter(grad_w_query, bits)
    key_value_sum = scatter(jnp.concatenate([grad_w_key, grad_w_value], axis=1), other)
    sum_key = key_value_sum[:, :head_dim]
    sum_value = key_value_sum[:, head_dim:]
    pieces = (grad_attn_gain, grad_mlp_gain, grad_b_query, grad_b_key, grad_b_value)
    flat = jnp.concatenate(pieces)
    padded = -(-flat.shape[0] // 1024) * 1024
    flat = jnp.pad(flat, (0, padded - flat.shape[0])).reshape(8, padded // 8)
    for bit in bits:
        flat = flat + swap(flat, "ctx", bit)
    flat = flat.reshape(padded)
    small = []
    begin = 0
    for piece in pieces:
        small.append(flat[begin : begin + piece.shape[0]])
        begin += piece.shape[0]
    return (
        mixed,
        grad_tokens,
        small[0],
        sum_query,
        small[2],
        sum_key,
        small[3],
        sum_value,
        small[4],
        sum_out,
        small[1],
        sum_gate,
        sum_up,
        sum_down,
    )


def solution(mesh):
    return jax.shard_map(
        shards,
        mesh=mesh,
        in_specs=(
            P("ctx", None),
            P(),
            P(None, "tp"),
            P("tp"),
            P(None, "tp"),
            P("tp"),
            P(None, "tp"),
            P("tp"),
            P("tp", None),
            P(),
            P(None, "tp"),
            P(None, "tp"),
            P("tp", None),
            P("ctx", None),
            P(),
            P(),
        ),
        out_specs=(
            P("ctx", None),
            P("ctx", None),
            P(),
            P("ctx", "tp"),
            P("tp"),
            P("ctx", "tp"),
            P("tp"),
            P("ctx", "tp"),
            P("tp"),
            P("tp", "ctx"),
            P(),
            P("ctx", "tp"),
            P("ctx", "tp"),
            P("tp", "ctx"),
        ),
        check_vma=False,
    )
```

profile of v0, /device:TPU:0, one launch (start us, length us, event | category | flops | bytes accessed | tf_op | source)
XLA Modules:
  0.0 295.8 jit_solution(7910923183508820870)
XLA Ops:
  10.0 4.0 %collective-permute-start = (bf16[2,128,128]{2,1,0:T(8,128)(2,1)}, bf16[2,128,128]{2,1,0:T(8,128)(2,1)S(1)}, u32[]{:S(2)}, u32[]{:S(2)}) collective-permute-start(bf16[2,128,128]{2,1,0:T(8,128)(2,1)} %get-tuple-element.37), channel_id=1, source_target_pairs={{0,16},{2,18},{4,20},{6,22},{8,24},{10,26},{12,28},{14,30},{16,0},... | collective-permute-start | bytes 196616 | tf_op jit(solution)/shard_map/ppermute | solution.py:52
  19.6 3.4 %collective-permute-done.1 = bf16[2,256,128]{2,1,0:T(8,128)(2,1)S(1)} collective-permute-done((bf16[2,256,128]{2,1,0:T(8,128)(2,1)S(1)}, bf16[2,256,128]{2,1,0:T(8,128)(2,1)S(1)}, u32[]{:S(2)}, u32[]{:S(2)}) %collective-permute-start.1) | collective-permute-done | bytes 131104 | tf_op jit(solution)/shard_map/ppermute | solution.py:52
  26.1 4.3 %collective-permute-done.2 = bf16[2,512,128]{2,1,0:T(8,128)(2,1)S(1)} collective-permute-done((bf16[2,512,128]{2,1,0:T(8,128)(2,1)}, bf16[2,512,128]{2,1,0:T(8,128)(2,1)S(1)}, u32[]{:S(2)}, u32[]{:S(2)}) %collective-permute-start.2) | collective-permute-done | bytes 262176 | tf_op jit(solution)/shard_map/ppermute | solution.py:52
  32.4 8.7 %collective-permute-done.3 = bf16[2,1024,128]{2,1,0:T(8,128)(2,1)S(1)} collective-permute-done((bf16[2,1024,128]{2,1,0:T(8,128)(2,1)S(1)}, bf16[2,1024,128]{2,1,0:T(8,128)(2,1)S(1)}, u32[]{:S(2)}, u32[]{:S(2)}) %collective-permute-start.3) | collective-permute-done | bytes 524320 | tf_op jit(solution)/shard_map/ppermute | solution.py:52
  41.2 6.3 %shard_map.272 = (f32[256,448]{1,0:T(8,128)S(1)}, bf16[256,448]{1,0:T(8,128)(2,1)S(1)}, f32[4,1,448]{2,1,0:T(1,128)S(1)}) custom-call(s32[32]{0:T(128)S(1)} %select_reduce_fusion.slot_ref, s32[4]{0:T(128)S(1)} %and_select_fusion.1.low_ref, s32[4]{0:T(128)S(1)} %fusion.47.high_ref, bf16[256,448]{1,0:T(8,128)(2,1)S(1)} %copy.170.q_ref, ...), custom_call_target="tpu_custom_call" | custom-call | flops 939524096 | bytes 4000000 | tf_op jit(solution)/shard_map/pallas_call | solution.py:229
  49.7 3.8 %fusion.59 = f32[256,2432]{1,0:T(8,128)S(1)} fusion(bf16[256,896]{1,0:T(8,128)(2,1)S(1)} %copy-done.11, bf16[2432,896]{1,0:T(8,128)(2,1)} %param.29), kind=kOutput, calls=%fused_computation.202 | convolution fusion | flops 1115684864 | bytes 7307264 | tf_op jit(solution)/shard_map/dot_general | solution.py:380
  55.1 3.9 %fusion.58 = f32[256,2432]{1,0:T(8,128)S(1)} fusion(bf16[256,896]{1,0:T(8,128)(2,1)S(1)} %multiply_convert_fusion.3, bf16[896,2432]{1,0:T(8,128)(2,1)} %param.28), kind=kOutput, calls=%fused_computation.201 | convolution fusion | flops 1115684864 | bytes 7307264 | tf_op jit(solution)/shard_map/dot_general | solution.py:372
  74.8 8.8 %collective-permute-start.28 = (bf16[8,56,2432]{2,1,0:T(8,128)(2,1)}, bf16[8,56,2432]{2,1,0:T(8,128)(2,1)}, u32[]{:S(2)}, u32[]{:S(2)}) collective-permute-start(bf16[8,56,2432]{2,1,0:T(8,128)(2,1)} %dynamic-slice_bitcast_fusion.2), channel_id=1, source_target_pairs={{0,2},{2,0},{4,6},{6,4},{8,10},{10,8},{12,14},{14,12},{16,18},{18,... | collective-permute-start | bytes 6537224 | tf_op jit(solution)/shard_map/ppermute | solution.py:52
  90.7 7.2 %shard_map.273 = (f32[256,448]{1,0:T(8,128)S(1)}, bf16[2,32,64,128]{3,2,1,0:T(8,128)(2,1)S(1)}) custom-call(s32[32]{0:T(128)S(1)} %select_reduce_fusion.slot_ref, s32[4]{0:T(128)S(1)} %and_select_fusion.1.low_ref, s32[4]{0:T(128)S(1)} %fusion.47.high_ref, s32[32]{0:T(128)S(1)} %eq.40.block_ref, bf16[256,448]{1,0:T(8,128)(2,1)S(1)} %copy.170.q_ref, ...), custom_call_target="tpu_custom_call" | custom-call | flops 2348810240 | bytes 8000000 | tf_op jit(solution)/shard_map/pallas_call | solution.py:250
  98.6 5.2 %reshape.374 = bf16[4,2,112,448]{2,1,0,3:T(2,128)(2,1)S(1)} reshape(bf16[896,448]{0,1:T(8,128)(2,1)} %convolution_convert_fusion.4) | data formatting | bytes 1605632 | tf_op jit(solution)/shard_map/reshape | solution.py:75
  111.2 3.2 %constant_dynamic-slice_fusion.6 = (bf16[4,1,112,448]{2,1,0,3:T(2,128)(2,1)}, bf16[4,1,112,448]{2,1,0,3:T(2,128)(2,1)}) fusion(bf16[4,2,112,448]{2,1,0,3:T(2,128)(2,1)S(1)} %reshape.374, s32[]{:T(128)S(6)} %select_n.203, s32[]{:T(128)S(6)} %select_n.204), kind=kLoop, calls=%fused_computation.161 | loop fusion | bytes 1605640 | tf_op jit(solution)/shard_map/jit(dynamic_index_in_dim)/dynamic_slice | solution.py:77
  114.3 3.4 %copy.202 = bf16[4,1,112,448]{3,2,0,1:T(8,128)(2,1)} copy(bf16[4,1,112,448]{2,1,0,3:T(2,128)(2,1)} %get-tuple-element.44) | data formatting | bytes 802816
  117.8 7.3 %collective-permute-start.24 = (bf16[4,112,448]{2,1,0:T(8,128)(2,1)}, bf16[4,112,448]{2,1,0:T(8,128)(2,1)}, u32[]{:S(2)}, u32[]{:S(2)}) collective-permute-start(bf16[4,112,448]{2,1,0:T(8,128)(2,1)} %bitcast.38), channel_id=1, source_target_pairs={{0,4},{2,6},{4,0},{6,2},{8,12},{10,14},{12,8},{14,10},{16,20},{18,... | collective-permute-start | bytes 1204232 | tf_op jit(solution)/shard_map/ppermute | solution.py:52
  127.5 3.7 %copy.201 = bf16[4,1,112,448]{3,2,0,1:T(8,128)(2,1)} copy(bf16[4,1,112,448]{2,1,0,3:T(2,128)(2,1)} %get-tuple-element.43) | data formatting | bytes 802816
  131.2 10.0 %collective-permute-done.16 = bf16[8,56,448]{2,1,0:T(8,128)(2,1)} collective-permute-done((bf16[8,56,448]{2,1,0:T(8,128)(2,1)}, bf16[8,56,448]{2,1,0:T(8,128)(2,1)}, u32[]{:S(2)}, u32[]{:S(2)}) %collective-permute-start.16) | collective-permute-done | bytes 401440 | tf_op jit(solution)/shard_map/ppermute | solution.py:52
  145.9 8.7 %collective-permute-done.7 = bf16[2,1024,128]{2,1,0:T(8,128)(2,1)S(1)} collective-permute-done((bf16[2,1024,128]{2,1,0:T(8,128)(2,1)}, bf16[2,1024,128]{2,1,0:T(8,128)(2,1)S(1)}, u32[]{:S(2)}, u32[]{:S(2)}) %collective-permute-start.7) | collective-permute-done | bytes 524320 | tf_op jit(solution)/shard_map/ppermute | solution.py:52
  157.0 5.7 %collective-permute-done.8 = bf16[2,512,128]{2,1,0:T(8,128)(2,1)S(1)} collective-permute-done((bf16[2,512,128]{2,1,0:T(8,128)(2,1)S(1)}, bf16[2,512,128]{2,1,0:T(8,128)(2,1)S(1)}, u32[]{:S(2)}, u32[]{:S(2)}) %collective-permute-start.8) | collective-permute-done | bytes 262176 | tf_op jit(solution)/shard_map/ppermute | solution.py:52
  165.0 4.1 %collective-permute-done.9 = bf16[2,256,128]{2,1,0:T(8,128)(2,1)S(1)} collective-permute-done((bf16[2,256,128]{2,1,0:T(8,128)(2,1)S(1)}, bf16[2,256,128]{2,1,0:T(8,128)(2,1)S(1)}, u32[]{:S(2)}, u32[]{:S(2)}) %collective-permute-start.9) | collective-permute-done | bytes 131104 | tf_op jit(solution)/shard_map/ppermute | solution.py:52
  169.1 4.7 %collective-permute-start.10 = (bf16[2,128,128]{2,1,0:T(8,128)(2,1)S(1)}, bf16[2,128,128]{2,1,0:T(8,128)(2,1)S(1)}, u32[]{:S(2)}, u32[]{:S(2)}) collective-permute-start(bf16[2,128,128]{2,1,0:T(8,128)(2,1)S(1)} %slice.123), channel_id=1, source_target_pairs={{0,16},{2,18},{4,20},{6,22},{8,24},{10,26},{12,28},{14,30},{16,0},... | collective-permute-start | bytes 196616 | tf_op jit(solution)/shard_map/ppermute | solution.py:52
  180.9 3.3 %collective-permute-start.19 = (bf16[1,56,448]{2,1,0:T(8,128)(2,1)S(1)}, bf16[1,56,448]{2,1,0:T(8,128)(2,1)S(1)}, u32[]{:S(2)}, u32[]{:S(2)}) collective-permute-start(bf16[1,56,448]{2,1,0:T(8,128)(2,1)S(1)} %constant_dynamic-slice_fusion.8), channel_id=1, source_target_pairs={{0,16},{2,18},{4,20},{6,22},{8,24},{10,26},{12,28},{14,30},{16,0},... | collective-permute-start | bytes 150536 | tf_op jit(solution)/shard_map/ppermute | solution.py:52
  191.3 2.7 collective-permute-done.13
  199.0 2.6 collective-permute-start.15
  213.3 3.3 %collective-permute-done.23 = bf16[1,56,128]{2,1,0:T(8,128)(2,1)S(1)} collective-permute-done((bf16[1,56,128]{2,1,0:T(8,128)(2,1)S(1)}, bf16[1,56,128]{2,1,0:T(8,128)(2,1)S(1)}, u32[]{:S(2)}, u32[]{:S(2)}) %collective-permute-start.23) | collective-permute-done | bytes 14368 | tf_op jit(solution)/shard_map/ppermute | solution.py:52
  217.3 2.9 fusion.1
  227.6 9.6 %collective-permute-done.33 = bf16[4,56,2432]{2,1,0:T(8,128)(2,1)S(1)} collective-permute-done((bf16[4,56,2432]{2,1,0:T(8,128)(2,1)S(1)}, bf16[4,56,2432]{2,1,0:T(8,128)(2,1)S(1)}, u32[]{:S(2)}, u32[]{:S(2)}) %collective-permute-start.33) | collective-permute-done | bytes 1089568 | tf_op jit(solution)/shard_map/ppermute | solution.py:52
  237.7 2.5 collective-permute-done.29
  240.8 26.1 %collective-permute-done.37 = bf16[1,224,2432]{2,1,0:T(8,128)(2,1)S(1)} collective-permute-done((bf16[1,224,2432]{2,1,0:T(8,128)(2,1)S(1)}, bf16[1,224,2432]{2,1,0:T(8,128)(2,1)S(1)}, u32[]{:S(2)}, u32[]{:S(2)}) %collective-permute-start.37) | collective-permute-done | bytes 1089568 | tf_op jit(solution)/shard_map/ppermute | solution.py:52
  268.5 2.5 collective-permute-done.34
  271.3 5.8 %collective-permute-done.30 = bf16[2,56,2432]{2,1,0:T(8,128)(2,1)S(1)} collective-permute-done((bf16[2,56,2432]{2,1,0:T(8,128)(2,1)S(1)}, bf16[2,56,2432]{2,1,0:T(8,128)(2,1)S(1)}, u32[]{:S(2)}, u32[]{:S(2)}) %collective-permute-start.30) | collective-permute-done | bytes 544800 | tf_op jit(solution)/shard_map/ppermute | solution.py:52
  277.3 4.0 %collective-permute-done.38 = bf16[2,56,2432]{2,1,0:T(8,128)(2,1)S(1)} collective-permute-done((bf16[2,56,2432]{2,1,0:T(8,128)(2,1)S(1)}, bf16[2,56,2432]{2,1,0:T(8,128)(2,1)S(1)}, u32[]{:S(2)}, u32[]{:S(2)}) %collective-permute-start.38) | collective-permute-done | bytes 544800 | tf_op jit(solution)/shard_map/ppermute | solution.py:52
  283.1 4.9 %collective-permute-done.35 = bf16[1,56,2432]{2,1,0:T(8,128)(2,1)S(1)} collective-permute-done((bf16[1,56,2432]{2,1,0:T(8,128)(2,1)S(1)}, bf16[1,56,2432]{2,1,0:T(8,128)(2,1)S(1)}, u32[]{:S(2)}, u32[]{:S(2)}) %collective-permute-start.35) | collective-permute-done | bytes 272416 | tf_op jit(solution)/shard_map/ppermute | solution.py:52
  288.9 4.8 %collective-permute-done.31 = bf16[1,56,2432]{2,1,0:T(8,128)(2,1)S(1)} collective-permute-done((bf16[1,56,2432]{2,1,0:T(8,128)(2,1)S(1)}, bf16[1,56,2432]{2,1,0:T(8,128)(2,1)S(1)}, u32[]{:S(2)}, u32[]{:S(2)}) %collective-permute-start.31) | collective-permute-done | bytes 272416 | tf_op jit(solution)/shard_map/ppermute | solution.py:52
  (284 shorter events, 112.2 us)
Async XLA Ops:
  10.0 7.9 %collective-permute-start = (bf16[2,128,128]{2,1,0:T(8,128)(2,1)}, bf16[2,128,128]{2,1,0:T(8,128)(2,1)S(1)}, u32[]{:S(2)}, u32[]{:S(2)}) collective-permute-start(bf16[2,128,128]{2,1,0:T(8,128)(2,1)} %get-tuple-element.37), channel_id=1, source_target_pairs={{0,16},{2,18},{4,20},{6,22},{8,24},{10,26},{12,28},{14,30},{16,0},... | collective-permute-start | bytes 196616 | tf_op jit(solution)/shard_map/ppermute | solution.py:52
  18.0 5.0 %collective-permute-start.1 = (bf16[2,256,128]{2,1,0:T(8,128)(2,1)S(1)}, bf16[2,256,128]{2,1,0:T(8,128)(2,1)S(1)}, u32[]{:S(2)}, u32[]{:S(2)}) collective-permute-start(bf16[2,256,128]{2,1,0:T(8,128)(2,1)S(1)} %pad_maximum_fusion.2), channel_id=1, source_target_pairs={{0,8},{2,10},{4,12},{6,14},{8,0},{10,2},{12,4},{14,6},{16,24},{18,... | collective-permute-start | bytes 393224 | tf_op jit(solution)/shard_map/ppermute | solution.py:52
  23.8 6.6 %collective-permute-start.2 = (bf16[2,512,128]{2,1,0:T(8,128)(2,1)}, bf16[2,512,128]{2,1,0:T(8,128)(2,1)S(1)}, u32[]{:S(2)}, u32[]{:S(2)}) collective-permute-start(bf16[2,512,128]{2,1,0:T(8,128)(2,1)} %pad_maximum_fusion.1), channel_id=1, source_target_pairs={{0,4},{2,6},{4,0},{6,2},{8,12},{10,14},{12,8},{14,10},{16,20},{18,... | collective-permute-start | bytes 786440 | tf_op jit(solution)/shard_map/ppermute | solution.py:52
  30.5 10.6 %collective-permute-start.3 = (bf16[2,1024,128]{2,1,0:T(8,128)(2,1)S(1)}, bf16[2,1024,128]{2,1,0:T(8,128)(2,1)S(1)}, u32[]{:S(2)}, u32[]{:S(2)}) collective-permute-start(bf16[2,1024,128]{2,1,0:T(8,128)(2,1)S(1)} %pad_maximum_fusion), channel_id=1, source_target_pairs={{0,2},{2,0},{4,6},{6,4},{8,10},{10,8},{12,14},{14,12},{16,18},{18,... | collective-permute-start | bytes 1572872 | tf_op jit(solution)/shard_map/ppermute | solution.py:52
  67.1 19.0 %collective-permute-start.5 = (bf16[256,896]{1,0:T(8,128)(2,1)S(1)}, bf16[256,896]{1,0:T(8,128)(2,1)S(1)}, u32[]{:S(2)}, u32[]{:S(2)}) collective-permute-start(bf16[256,896]{1,0:T(8,128)(2,1)S(1)} %convolution_convert_fusion.5), channel_id=1, source_target_pairs={{0,1},{1,0},{2,3},{3,2},{4,5},{5,4},{6,7},{7,6},{8,9},{9,8},{10,11... | collective-permute-start | bytes 1376264 | tf_op jit(solution)/shard_map/ppermute | solution.py:52
  70.9 14.7 %collective-permute-start.6 = (bf16[256,896]{1,0:T(8,128)(2,1)S(1)}, bf16[256,896]{1,0:T(8,128)(2,1)S(1)}, u32[]{:S(2)}, u32[]{:S(2)}) collective-permute-start(bf16[256,896]{1,0:T(8,128)(2,1)S(1)} %fusion.7), channel_id=1, source_target_pairs={{0,1},{1,0},{2,3},{3,2},{4,5},{5,4},{6,7},{7,6},{8,9},{9,8},{10,11... | collective-permute-start | bytes 1376264 | tf_op jit(solution)/shard_map/ppermute | solution.py:52
  72.8 144.5 %collective-permute-start.32 = (bf16[4,112,2432]{2,1,0:T(8,128)(2,1)}, bf16[4,112,2432]{2,1,0:T(8,128)(2,1)}, u32[]{:S(2)}, u32[]{:S(2)}) collective-permute-start(bf16[4,112,2432]{2,1,0:T(8,128)(2,1)} %dynamic-slice_bitcast_fusion.1), channel_id=1, source_target_pairs={{0,4},{2,6},{4,0},{6,2},{8,12},{10,14},{12,8},{14,10},{16,20},{18,... | collective-permute-start | bytes 6537224 | tf_op jit(solution)/shard_map/ppermute | solution.py:52
  74.8 147.3 %collective-permute-start.28 = (bf16[8,56,2432]{2,1,0:T(8,128)(2,1)}, bf16[8,56,2432]{2,1,0:T(8,128)(2,1)}, u32[]{:S(2)}, u32[]{:S(2)}) collective-permute-start(bf16[8,56,2432]{2,1,0:T(8,128)(2,1)} %dynamic-slice_bitcast_fusion.2), channel_id=1, source_target_pairs={{0,2},{2,0},{4,6},{6,4},{8,10},{10,8},{12,14},{14,12},{16,18},{18,... | collective-permute-start | bytes 6537224 | tf_op jit(solution)/shard_map/ppermute | solution.py:52
  85.0 140.3 %collective-permute-start.36 = (bf16[2,224,2432]{2,1,0:T(8,128)(2,1)}, bf16[2,224,2432]{2,1,0:T(8,128)(2,1)}, u32[]{:S(2)}, u32[]{:S(2)}) collective-permute-start(bf16[2,224,2432]{2,1,0:T(8,128)(2,1)} %dynamic-slice_bitcast_fusion), channel_id=1, source_target_pairs={{0,8},{2,10},{4,12},{6,14},{8,0},{10,2},{12,4},{14,6},{16,24},{18,... | collective-permute-start | bytes 6537224 | tf_op jit(solution)/shard_map/ppermute | solution.py:52
  110.3 30.9 %collective-permute-start.16 = (bf16[8,56,448]{2,1,0:T(8,128)(2,1)}, bf16[8,56,448]{2,1,0:T(8,128)(2,1)}, u32[]{:S(2)}, u32[]{:S(2)}) collective-permute-start(bf16[8,56,448]{2,1,0:T(8,128)(2,1)} %dynamic-slice_bitcast_fusion.8), channel_id=1, source_target_pairs={{0,2},{2,0},{4,6},{6,4},{8,10},{10,8},{12,14},{14,12},{16,18},{18,... | collective-permute-start | bytes 1204232 | tf_op jit(solution)/shard_map/ppermute | solution.py:52
  117.8 26.5 %collective-permute-start.24 = (bf16[4,112,448]{2,1,0:T(8,128)(2,1)}, bf16[4,112,448]{2,1,0:T(8,128)(2,1)}, u32[]{:S(2)}, u32[]{:S(2)}) collective-permute-start(bf16[4,112,448]{2,1,0:T(8,128)(2,1)} %bitcast.38), channel_id=1, source_target_pairs={{0,4},{2,6},{4,0},{6,2},{8,12},{10,14},{12,8},{14,10},{16,20},{18,... | collective-permute-start | bytes 1204232 | tf_op jit(solution)/shard_map/ppermute | solution.py:52
  141.2 13.5 %collective-permute-start.7 = (bf16[2,1024,128]{2,1,0:T(8,128)(2,1)}, bf16[2,1024,128]{2,1,0:T(8,128)(2,1)S(1)}, u32[]{:S(2)}, u32[]{:S(2)}) collective-permute-start(bf16[2,1024,128]{2,1,0:T(8,128)(2,1)} %slice.117), channel_id=1, source_target_pairs={{0,2},{2,0},{4,6},{6,4},{8,10},{10,8},{12,14},{14,12},{16,18},{18,... | collective-permute-start | bytes 1572872 | tf_op jit(solution)/shard_map/ppermute | solution.py:52
  144.2 12.0 %collective-permute-start.17 = (bf16[4,56,448]{2,1,0:T(8,128)(2,1)S(1)}, bf16[4,56,448]{2,1,0:T(8,128)(2,1)S(1)}, u32[]{:S(2)}, u32[]{:S(2)}) collective-permute-start(bf16[4,56,448]{2,1,0:T(8,128)(2,1)S(1)} %dynamic-slice_bitcast_fusion.10), channel_id=1, source_target_pairs={{0,4},{2,6},{4,0},{6,2},{8,12},{10,14},{12,8},{14,10},{16,20},{18,... | collective-permute-start | bytes 602120 | tf_op jit(solution)/shard_map/ppermute | solution.py:52
  154.6 9.4 %collective-permute-start.25 = (bf16[4,56,448]{2,1,0:T(8,128)(2,1)S(1)}, bf16[4,56,448]{2,1,0:T(8,128)(2,1)S(1)}, u32[]{:S(2)}, u32[]{:S(2)}) collective-permute-start(bf16[4,56,448]{2,1,0:T(8,128)(2,1)S(1)} %dynamic-slice_bitcast_fusion.9), channel_id=1, source_target_pairs={{0,2},{2,0},{4,6},{6,4},{8,10},{10,8},{12,14},{14,12},{16,18},{18,... | collective-permute-start | bytes 602120 | tf_op jit(solution)/shard_map/ppermute | solution.py:52
  156.3 6.4 %collective-permute-start.8 = (bf16[2,512,128]{2,1,0:T(8,128)(2,1)S(1)}, bf16[2,512,128]{2,1,0:T(8,128)(2,1)S(1)}, u32[]{:S(2)}, u32[]{:S(2)}) collective-permute-start(bf16[2,512,128]{2,1,0:T(8,128)(2,1)S(1)} %slice.119), channel_id=1, source_target_pairs={{0,4},{2,6},{4,0},{6,2},{8,12},{10,14},{12,8},{14,10},{16,20},{18,... | collective-permute-start | bytes 786440 | tf_op jit(solution)/shard_map/ppermute | solution.py:52
  162.7 16.2 %collective-permute-start.18 = (bf16[2,56,448]{2,1,0:T(8,128)(2,1)S(1)}, bf16[2,56,448]{2,1,0:T(8,128)(2,1)S(1)}, u32[]{:S(2)}, u32[]{:S(2)}) collective-permute-start(bf16[2,56,448]{2,1,0:T(8,128)(2,1)S(1)} %dynamic-slice_bitcast_fusion.12), channel_id=1, source_target_pairs={{0,8},{2,10},{4,12},{6,14},{8,0},{10,2},{12,4},{14,6},{16,24},{18,... | collective-permute-start | bytes 301064 | tf_op jit(solution)/shard_map/ppermute | solution.py:52
  164.0 5.0 %collective-permute-start.9 = (bf16[2,256,128]{2,1,0:T(8,128)(2,1)S(1)}, bf16[2,256,128]{2,1,0:T(8,128)(2,1)S(1)}, u32[]{:S(2)}, u32[]{:S(2)}) collective-permute-start(bf16[2,256,128]{2,1,0:T(8,128)(2,1)S(1)} %slice.121), channel_id=1, source_target_pairs={{0,8},{2,10},{4,12},{6,14},{8,0},{10,2},{12,4},{14,6},{16,24},{18,... | collective-permute-start | bytes 393224 | tf_op jit(solution)/shard_map/ppermute | solution.py:52
  169.1 7.0 %collective-permute-start.10 = (bf16[2,128,128]{2,1,0:T(8,128)(2,1)S(1)}, bf16[2,128,128]{2,1,0:T(8,128)(2,1)S(1)}, u32[]{:S(2)}, u32[]{:S(2)}) collective-permute-start(bf16[2,128,128]{2,1,0:T(8,128)(2,1)S(1)} %slice.123), channel_id=1, source_target_pairs={{0,16},{2,18},{4,20},{6,22},{8,24},{10,26},{12,28},{14,30},{16,0},... | collective-permute-start | bytes 196616 | tf_op jit(solution)/shard_map/ppermute | solution.py:52
  178.9 5.4 %collective-permute-start.11 = (bf16[256,896]{1,0:T(8,128)(2,1)S(1)}, bf16[256,896]{1,0:T(8,128)(2,1)S(1)}, u32[]{:S(2)}, u32[]{:S(2)}) collective-permute-start(bf16[256,896]{1,0:T(8,128)(2,1)S(1)} %fusion.6), channel_id=1, source_target_pairs={{0,1},{1,0},{2,3},{3,2},{4,5},{5,4},{6,7},{7,6},{8,9},{9,8},{10,11... | collective-permute-start | bytes 1376264 | tf_op jit(solution)/shard_map/ppermute | solution.py:52
  180.9 14.1 %collective-permute-start.19 = (bf16[1,56,448]{2,1,0:T(8,128)(2,1)S(1)}, bf16[1,56,448]{2,1,0:T(8,128)(2,1)S(1)}, u32[]{:S(2)}, u32[]{:S(2)}) collective-permute-start(bf16[1,56,448]{2,1,0:T(8,128)(2,1)S(1)} %constant_dynamic-slice_fusion.8), channel_id=1, source_target_pairs={{0,16},{2,18},{4,20},{6,22},{8,24},{10,26},{12,28},{14,30},{16,0},... | collective-permute-start | bytes 150536 | tf_op jit(solution)/shard_map/ppermute | solution.py:52
  194.0 5.0 %collective-permute-start.20 = (bf16[4,112,128]{1,2,0:T(8,128)(2,1)S(1)}, bf16[4,112,128]{1,2,0:T(8,128)(2,1)S(1)}, u32[]{:S(2)}, u32[]{:S(2)}) collective-permute-start(bf16[4,112,128]{1,2,0:T(8,128)(2,1)S(1)} %fusion.38), channel_id=1, source_target_pairs={{0,4},{2,6},{4,0},{6,2},{8,12},{10,14},{12,8},{14,10},{16,20},{18,... | collective-permute-start | bytes 344072 | tf_op jit(solution)/shard_map/ppermute | solution.py:52
  198.6 5.1 %collective-permute-start.27 = (bf16[1,56,448]{2,1,0:T(8,128)(2,1)S(1)}, bf16[1,56,448]{2,1,0:T(8,128)(2,1)S(1)}, u32[]{:S(2)}, u32[]{:S(2)}) collective-permute-start(bf16[1,56,448]{2,1,0:T(8,128)(2,1)S(1)} %constant_dynamic-slice_fusion.4), channel_id=1, source_target_pairs={{0,16},{2,18},{4,20},{6,22},{8,24},{10,26},{12,28},{14,30},{16,0},... | collective-permute-start | bytes 150536 | tf_op jit(solution)/shard_map/ppermute | solution.py:52
  199.0 7.1 %collective-permute-start.15 = (f32[8,384]{1,0:T(8,128)S(1)}, f32[8,384]{1,0:T(8,128)S(1)}, u32[]{:S(2)}, u32[]{:S(2)}) collective-permute-start(f32[8,384]{1,0:T(8,128)S(1)} %add.382), channel_id=1, source_target_pairs={{0,16},{2,18},{4,20},{6,22},{8,24},{10,26},{12,28},{14,30},{16,0},... | collective-permute-start | bytes 36872 | tf_op jit(solution)/shard_map/ppermute | solution.py:52
  220.4 16.9 %collective-permute-start.33 = (bf16[4,56,2432]{2,1,0:T(8,128)(2,1)S(1)}, bf16[4,56,2432]{2,1,0:T(8,128)(2,1)S(1)}, u32[]{:S(2)}, u32[]{:S(2)}) collective-permute-start(bf16[4,56,2432]{2,1,0:T(8,128)(2,1)S(1)} %dynamic-slice_bitcast_fusion.3), channel_id=1, source_target_pairs={{0,2},{2,0},{4,6},{6,4},{8,10},{10,8},{12,14},{14,12},{16,18},{18,... | collective-permute-start | bytes 3268616 | tf_op jit(solution)/shard_map/ppermute | solution.py:52
  224.3 15.9 %collective-permute-start.29 = (bf16[4,56,2432]{2,1,0:T(8,128)(2,1)S(1)}, bf16[4,56,2432]{2,1,0:T(8,128)(2,1)S(1)}, u32[]{:S(2)}, u32[]{:S(2)}) collective-permute-start(bf16[4,56,2432]{2,1,0:T(8,128)(2,1)S(1)} %dynamic-slice_bitcast_fusion.4), channel_id=1, source_target_pairs={{0,4},{2,6},{4,0},{6,2},{8,12},{10,14},{12,8},{14,10},{16,20},{18,... | collective-permute-start | bytes 3268616 | tf_op jit(solution)/shard_map/ppermute | solution.py:52
  227.6 39.3 %collective-permute-start.37 = (bf16[1,224,2432]{2,1,0:T(8,128)(2,1)S(1)}, bf16[1,224,2432]{2,1,0:T(8,128)(2,1)S(1)}, u32[]{:S(2)}, u32[]{:S(2)}) collective-permute-start(bf16[1,224,2432]{2,1,0:T(8,128)(2,1)S(1)} %constant_dynamic-slice_fusion.1), channel_id=1, source_target_pairs={{0,16},{2,18},{4,20},{6,22},{8,24},{10,26},{12,28},{14,30},{16,0},... | collective-permute-start | bytes 3268616 | tf_op jit(solution)/shard_map/ppermute | solution.py:52
  237.6 33.4 %collective-permute-start.34 = (bf16[2,56,2432]{2,1,0:T(8,128)(2,1)S(1)}, bf16[2,56,2432]{2,1,0:T(8,128)(2,1)S(1)}, u32[]{:S(2)}, u32[]{:S(2)}) collective-permute-start(bf16[2,56,2432]{2,1,0:T(8,128)(2,1)S(1)} %dynamic-slice_bitcast_fusion.6), channel_id=1, source_target_pairs={{0,8},{2,10},{4,12},{6,14},{8,0},{10,2},{12,4},{14,6},{16,24},{18,... | collective-permute-start | bytes 1634312 | tf_op jit(solution)/shard_map/ppermute | solution.py:52
  240.5 36.5 %collective-permute-start.30 = (bf16[2,56,2432]{2,1,0:T(8,128)(2,1)S(1)}, bf16[2,56,2432]{2,1,0:T(8,128)(2,1)S(1)}, u32[]{:S(2)}, u32[]{:S(2)}) collective-permute-start(bf16[2,56,2432]{2,1,0:T(8,128)(2,1)S(1)} %dynamic-slice_bitcast_fusion.7), channel_id=1, source_target_pairs={{0,8},{2,10},{4,12},{6,14},{8,0},{10,2},{12,4},{14,6},{16,24},{18,... | collective-permute-start | bytes 1634312 | tf_op jit(solution)/shard_map/ppermute | solution.py:52
  267.3 14.1 %collective-permute-start.38 = (bf16[2,56,2432]{2,1,0:T(8,128)(2,1)S(1)}, bf16[2,56,2432]{2,1,0:T(8,128)(2,1)S(1)}, u32[]{:S(2)}, u32[]{:S(2)}) collective-permute-start(bf16[2,56,2432]{2,1,0:T(8,128)(2,1)S(1)} %dynamic-slice_bitcast_fusion.5), channel_id=1, source_target_pairs={{0,2},{2,0},{4,6},{6,4},{8,10},{10,8},{12,14},{14,12},{16,18},{18,... | collective-permute-start | bytes 1634312 | tf_op jit(solution)/shard_map/ppermute | solution.py:52
  271.2 16.9 %collective-permute-start.35 = (bf16[1,56,2432]{2,1,0:T(8,128)(2,1)S(1)}, bf16[1,56,2432]{2,1,0:T(8,128)(2,1)S(1)}, u32[]{:S(2)}, u32[]{:S(2)}) collective-permute-start(bf16[1,56,2432]{2,1,0:T(8,128)(2,1)S(1)} %constant_dynamic-slice_fusion.2), channel_id=1, source_target_pairs={{0,16},{2,18},{4,20},{6,22},{8,24},{10,26},{12,28},{14,30},{16,0},... | collective-permute-start | bytes 817160 | tf_op jit(solution)/shard_map/ppermute | solution.py:52
  277.3 16.4 %collective-permute-start.31 = (bf16[1,56,2432]{2,1,0:T(8,128)(2,1)S(1)}, bf16[1,56,2432]{2,1,0:T(8,128)(2,1)S(1)}, u32[]{:S(2)}, u32[]{:S(2)}) collective-permute-start(bf16[1,56,2432]{2,1,0:T(8,128)(2,1)S(1)} %constant_dynamic-slice_fusion.3), channel_id=1, source_target_pairs={{0,16},{2,18},{4,20},{6,22},{8,24},{10,26},{12,28},{14,30},{16,0},... | collective-permute-start | bytes 817160 | tf_op jit(solution)/shard_map/ppermute | solution.py:52
  281.6 13.0 %collective-permute-start.39 = (bf16[1,56,2432]{2,1,0:T(8,128)(2,1)S(1)}, bf16[1,56,2432]{2,1,0:T(8,128)(2,1)S(1)}, u32[]{:S(2)}, u32[]{:S(2)}) collective-permute-start(bf16[1,56,2432]{2,1,0:T(8,128)(2,1)S(1)} %constant_dynamic-slice_fusion), channel_id=1, source_target_pairs={{0,4},{2,6},{4,0},{6,2},{8,12},{10,14},{12,8},{14,10},{16,20},{18,... | collective-permute-start | bytes 817160 | tf_op jit(solution)/shard_map/ppermute | solution.py:52
  (38 other events, 320.4 us)
where the time goes:
time: 300 us; the launch traced here: 296 us
  waiting for transfers between devices  126 us (42%)
  starting transfers between devices  59.6 us (20%)
  local copies, waits for them, and re-layouts  34.6 us (12%)
  matrix products  30.3 us (10%)
  other arithmetic  29.8 us (10%)
  Pallas kernels  13.5 us (4%)
    ppermute x40, waiting for transfers between devices, swap(): return lax.ppermute(values, axis_name, [(i, i ^ bit) for i in range(size)])  126 us
    ppermute x40, starting transfers between devices, swap(): return lax.ppermute(values, axis_name, [(i, i ^ bit) for i in range(size)])  59.6 us
    convert_element_type x18, other arithmetic, scatter_rows(): cur = total.astype(jnp.bfloat16).reshape(before * after * block, columns)  11.2 us
    unnamed x66, local copies, waits for them, and re-layouts  9.92 us
    pallas_call x1, Pallas kernels, backward(): pl.pallas_call(functools.partial(backward_kernel, key_len, head_dim ** (-...  7.18 us
    squeeze x22, local copies, waits for them, and re-layouts, scatter_rows(): send = lax.dynamic_index_in_dim(shaped, 1 - mine, 1, keepdims=False)  7.07 us
    pallas_call x1, Pallas kernels, forward(): pl.pallas_call(functools.partial(forward_kernel, key_len), grid_spec=pltp...  6.28 us
  transfers between devices with their start and end apart: 40, of which 26 were waited for; matrix products, arithmetic and copies ran while one was open for 22% of the time, Pallas kernels for 2%

commit v1 on v0

--- a/solution.py
+++ b/solution.py
@@ -61,29 +61,39 @@
     return [1 << b for b in range(count.bit_length() - 1)]
 
 
-def scatter_rows(matrix, order):
-    index = lax.axis_index("ctx")
-    count = lax.axis_size("ctx")
-    rows, columns = matrix.shape
-    block = rows // count
-    cur = matrix
-    left = sorted(order, reverse=True)
-    for bit in order:
+class RowScatter:
+    def __init__(self, matrix, order):
+        self.cur = matrix.astype(jnp.bfloat16)
+        self.order = list(order)
+        self.block = matrix.shape[0] // lax.axis_size("ctx")
+        self.columns = matrix.shape[1]
+
+    def stage(self):
+        bit = self.order.pop(0)
+        left = sorted(self.order + [bit], reverse=True)
         at = left.index(bit)
         before = 1 << at
         after = 1 << (len(left) - at - 1)
-        shaped = cur.reshape(before, 2, after * block, columns)
-        mine = (index // bit) % 2
+        shaped = self.cur.reshape(before, 2, after * self.block, self.columns)
+        mine = (lax.axis_index("ctx") // bit) % 2
         keep = lax.dynamic_index_in_dim(shaped, mine, 1, keepdims=False)
         send = lax.dynamic_index_in_dim(shaped, 1 - mine, 1, keepdims=False)
         got = swap(send, "ctx", bit)
         total = keep.astype(jnp.float32) + got.astype(jnp.float32)
-        left.remove(bit)
-        if left:
-            cur = total.astype(jnp.bfloat16).reshape(before * after * block, columns)
-        else:
-            cur = total.reshape(block, columns)
-    return cur
+        total = total.reshape(before * after * self.block, self.columns)
+        self.cur = total.astype(jnp.bfloat16) if self.order else total
+
+    def finish(self):
+        while self.order:
+            self.stage()
+        return self.cur
+
+
+def in_step(flows, *others):
+    held = lax.optimization_barrier(tuple(flow.cur for flow in flows) + others)
+    for flow, cur in zip(flows, held):
+        flow.cur = cur
+    return held[len(flows) :]
 
 
 def stack_heads(rows, head_dim):
@@ -159,7 +169,7 @@
 
 def backward_kernel(
     key_len, scale, slot_ref, low_ref, high_ref, block_ref, q_ref, kv_ref, pos_ref, first_ref,
-    attn_ref, log_ref, grad_ref, grad_q_ref, grad_kv_ref, sorted_ref, acc_ref,
+    attn_ref, log_ref, grad_ref, cos_ref, sin_ref, grad_q_ref, grad_kv_ref, sorted_ref, acc_ref,
 ):
     step = pl.program_id(0) * pl.num_programs(1) + pl.program_id(1)
     head_dim = kv_ref.shape[3] // 2
@@ -202,7 +212,13 @@
     grad_q = lax.fori_loop(
         low_ref[step], high_ref[step], body, jnp.zeros((head_dim, rows), jnp.float32)
     )
-    grad_q_ref[...] = unstack_heads(grad_q.T, count) * scale
+    half = head_dim // 2
+    upper, lower = grad_q[:half] * scale, grad_q[half:] * scale
+    cos_part, sin_part = cos_ref[0], sin_ref[0]
+    turned = jnp.concatenate(
+        [upper * cos_part + lower * sin_part, lower * cos_part - upper * sin_part], axis=0
+    )
+    grad_q_ref[...] = unstack_heads(turned.T, count).astype(jnp.bfloat16)
 
     @pl.when(pl.program_id(1) == pl.num_programs(1) - 1)
     def _():
@@ -214,13 +230,14 @@
         lax.fori_loop(0, blocks, move, 0)
 
 
-def attention(seq_count, key_len, head_dim, plan, queries, key_values, pos, first):
+def attention(seq_count, key_len, head_dim, plan, queries, key_values, pos, first, turns):
     rows, width = queries.shape
     blocks, block_len = key_values.shape[1:3]
     stacked = pos.shape[2]
     row_spec = pl.BlockSpec((block_len, width), lambda s, j, *_: (s * 2 + j, 0))
     kv_spec = pl.BlockSpec((1, blocks, block_len, 2 * head_dim), lambda s, j, *_: (s, 0, 0, 0))
     lane_spec = pl.BlockSpec((1, 1, stacked), lambda s, j, *_: (s * 2 + j, 0, 0))
+    turn_spec = pl.BlockSpec((1, head_dim // 2, stacked), lambda s, j, *_: (j, 0, 0))
     flops = 2 * 2 * rows * width * blocks * block_len // 2
     sorted_shape = pltpu.VMEM((blocks * block_len, 2 * head_dim), jnp.bfloat16)
     params = pltpu.CompilerParams(vmem_limit_bytes=VMEM_BYTES)
@@ -252,7 +269,8 @@
             grid_spec=pltpu.PrefetchScalarGridSpec(
                 num_scalar_prefetch=4,
                 grid=(seq_count, 2),
-                in_specs=[row_spec, kv_spec, lane_spec, lane_spec, row_spec, lane_spec, row_spec],
+                in_specs=[row_spec, kv_spec, lane_spec, lane_spec, row_spec, lane_spec, row_spec,
+                          turn_spec, turn_spec],
                 out_specs=[row_spec, kv_spec],
                 scratch_shapes=[
                     sorted_shape,
@@ -260,14 +278,14 @@
                 ],
             ),
             out_shape=[
-                jax.ShapeDtypeStruct((rows, width), jnp.float32),
+                jax.ShapeDtypeStruct((rows, width), jnp.bfloat16),
                 jax.ShapeDtypeStruct(key_values.shape, jnp.bfloat16),
             ],
             compiler_params=params,
             cost_estimate=pl.CostEstimate(
                 flops=flops * 5, bytes_accessed=8000000, transcendentals=flops // 128
             ),
-        )(*plan, queries, key_values, pos, first, attended, log_total, grads)
+        )(*plan, queries, key_values, pos, first, attended, log_total, grads, *turns)
 
     return forward, backward
 
@@ -325,6 +343,10 @@
         own_pos.reshape(1, 2, block_len), (seq_count, 2, block_len)
     ).reshape(2 * seq_count, block_len)
     first_blocks = own_first.reshape(2 * seq_count, block_len)
+    turns = [
+        jnp.tile(table.reshape(2, block_len, head_dim // 2).transpose(0, 2, 1), (1, 1, group))
+        for table in (cos_table, sin_table)
+    ]
     plan = (
         block_slots,
         first_blocks[:, 0] // key_len,
@@ -361,7 +383,7 @@
         gathered = jnp.concatenate([gathered, swap(gathered, "ctx", bit)], axis=1)
     key_values = gathered.reshape(seq_count, 2 * ctx_size, block_len, 2 * head_dim)
     attend, attend_back = attention(
-        seq_count, key_len, head_dim, plan, query_low, key_values, lane_pos, lane_first
+        seq_count, key_len, head_dim, plan, query_low, key_values, lane_pos, lane_first, turns
     )
     attended, attn_low, log_total = attend()
     branch = sum_pair(jnp.dot(attn_low, w_out, preferred_element_type=jnp.float32))
@@ -395,7 +417,16 @@
     grad_attn_low = jnp.dot(grad_branch, w_out.T, preferred_element_type=jnp.float32).astype(
         jnp.bfloat16
     )
-    grad_query_rows, grad_key_values = attend_back(attended, log_total, grad_attn_low)
+    other = [bits[1], bits[0]] + bits[2:]
+    last = bits[2:] + bits[:2]
+    flow_down = RowScatter(grad_w_down, last)
+    flow_gate = RowScatter(grad_w_gate, bits)
+    flow_up = RowScatter(grad_w_up, other)
+    flow_out = RowScatter(grad_w_out, other)
+    flows = [flow_down, flow_gate, flow_up, flow_out]
+    for flow in flows:
+        flow.stage()
+    grad_query_low, grad_key_values = attend_back(attended, log_total, grad_attn_low)
     cur = grad_key_values.reshape(seq_count, seq_len, 2 * head_dim)
     for bit in bits:
         half = cur.shape[1] // 2
@@ -403,21 +434,23 @@
             jnp.float32
         )
         cur = total if bit == bits[-1] else total.astype(jnp.bfloat16)
+        if bit == bits[0]:
+            (cur,) = in_step(flows, cur)
+            for flow in flows:
+                flow.stage()
     grad_keys_own = cur[:, :, :head_dim]
     grad_values_own = cur[:, :, head_dim:]
-    grad_query_rows = grad_query_rows.reshape(seq_count, half_rows, group, head_dim)
-    grad_query_low = (
-        rotate(grad_query_rows, cos_table, -sin_table)
-        .reshape(tok_rows, group * head_dim)
-        .astype(jnp.bfloat16)
-    )
+    flow_query = RowScatter(
+        jnp.dot(normed.T, grad_query_low, preferred_element_type=jnp.float32), bits
+    )
+    flow_query.stage()
+    flow_query.stage()
     grad_key_low = (
         rotate(grad_keys_own.reshape(seq_count, half_rows, 1, head_dim), cos_table, -sin_table)
         .reshape(tok_rows, head_dim)
         .astype(jnp.bfloat16)
     )
     grad_value_low = grad_values_own.reshape(tok_rows, head_dim).astype(jnp.bfloat16)
-    grad_w_query = jnp.dot(normed.T, grad_query_low, preferred_element_type=jnp.float32)
     grad_w_key = jnp.dot(normed.T, grad_key_low, preferred_element_type=jnp.float32)
     grad_w_value = jnp.dot(normed.T, grad_value_low, preferred_element_type=jnp.float32)
     grad_b_query = jnp.sum(grad_query_low.astype(jnp.float32), axis=0)
@@ -428,21 +461,26 @@
         + jnp.dot(grad_key_low, w_key.T, preferred_element_type=jnp.float32)
         + jnp.dot(grad_value_low, w_value.T, preferred_element_type=jnp.float32)
     )
-    grad_normed = sum_pair(grad_first_part)
+    flows = flows + [flow_query]
+    grad_w_pair = jnp.concatenate([grad_w_key, grad_w_value], axis=1).astype(jnp.bfloat16)
+    first_low, grad_w_pair = in_step(
+        flows, grad_first_part.astype(jnp.bfloat16), grad_w_pair
+    )
+    for flow in flows:
+        flow.stage()
+    flow_pair = RowScatter(grad_w_pair, other)
+    flow_pair.stage()
+    flow_pair.stage()
+    grad_normed = sum_pair(first_low)
     grad_in_part, grad_attn_gain = norm_back(grad_normed, x_float, inv_one, gain_one)
     grad_tokens = grad_stream + grad_in_part
-    other = [bits[1], bits[0]] + bits[2:]
-
-    def scatter(matrix, order):
-        return scatter_rows(matrix.astype(jnp.bfloat16), order)
-
-    last = bits[2:] + bits[:2]
-    sum_down = scatter(grad_w_down, last).T
-    sum_gate = scatter(grad_w_gate, bits)
-    sum_up = scatter(grad_w_up, other)
-    sum_out = scatter(grad_w_out, other).T
-    sum_query = scatter(grad_w_query, bits)
-    key_value_sum = scatter(jnp.concatenate([grad_w_key, grad_w_value], axis=1), other)
+    in_step(flows + [flow_pair])
+    sum_down = flow_down.finish().T
+    sum_gate = flow_gate.finish()
+    sum_up = flow_up.finish()
+    sum_out = flow_out.finish().T
+    sum_query = flow_query.finish()
+    key_value_sum = flow_pair.finish()
     sum_key = key_value_sum[:, :head_dim]
     sum_value = key_value_sum[:, head_dim:]
     pieces = (grad_attn_gain, grad_mlp_gain, grad_b_query, grad_b_key, grad_b_value)

time: 300 us -> 315 us (1.050); the launches traced: 296 us -> 315 us
  other arithmetic: 29.8 us -> 37 us
  local copies, waits for them, and re-layouts: 34.6 us -> 41.7 us
  Pallas kernels: 13.5 us -> 20.1 us
  starting transfers between devices: 59.6 us -> 55.6 us
    convert_element_type x18, other arithmetic: 11.2 us -> 18.3 us  [stage(): self.cur = total.astype(jnp.bfloat16) if self.order else total]
    ppermute x40, starting transfers between devices: 59.6 us -> 55.6 us  [swap(): return lax.ppermute(values, axis_name, [(i, i ^ bit) for i in range(size)])]
    squeeze x22 -> x23, local copies, waits for them, and re-layouts: 7.07 us -> 10.5 us  [stage(): send = lax.dynamic_index_in_dim(shaped, 1 - mine, 1, keepdims=False)]
    pallas_call x1, Pallas kernels: 6.28 us -> 9.65 us  [forward(): pl.pallas_call(functools.partial(forward_kernel, key_len), grid_spec=pltp...]
    pallas_call x1, Pallas kernels: 7.18 us -> 10.5 us  [backward(): pl.pallas_call(functools.partial(backward_kernel, key_len, head_dim ** (-...]
    unnamed x66 -> x80, local copies, waits for them, and re-layouts: 9.92 us -> 10.1 us
  transfers between devices with their start and end apart: 40 -> 40, of which waited for: 26 -> 16; matrix products, arithmetic and copies ran while one was open for 22% -> 23% of each run, Pallas kernels for 2% -> 3%
where the time goes in v1:
time: 315 us
  waiting for transfers between devices  128 us (41%)
  starting transfers between devices  55.6 us (18%)
  local copies, waits for them, and re-layouts  41.7 us (13%)
  other arithmetic  37 us (12%)
  matrix products  30 us (10%)
  Pallas kernels  20.1 us (6%)
    ppermute x40, waiting for transfers between devices, swap(): return lax.ppermute(values, axis_name, [(i, i ^ bit) for i in range(size)])  128 us
    ppermute x40, starting transfers between devices, swap(): return lax.ppermute(values, axis_name, [(i, i ^ bit) for i in range(size)])  55.6 us
    convert_element_type x18, other arithmetic, stage(): self.cur = total.astype(jnp.bfloat16) if self.order else total  18.3 us
    squeeze x23, local copies, waits for them, and re-layouts, stage(): send = lax.dynamic_index_in_dim(shaped, 1 - mine, 1, keepdims=False)  10.5 us
    pallas_call x1, Pallas kernels, backward(): pl.pallas_call(functools.partial(backward_kernel, key_len, head_dim ** (-...  10.5 us
    unnamed x80, local copies, waits for them, and re-layouts  10.1 us
    pallas_call x1, Pallas kernels, forward(): pl.pallas_call(functools.partial(forward_kernel, key_len), grid_spec=pltp...  9.65 us
  transfers between devices with their start and end apart: 40, of which 16 were waited for; matrix products, arithmetic and copies ran while one was open for 23% of the time, Pallas kernels for 3%

profile of v1, /device:TPU:0, one launch (start us, length us, event | category | flops | bytes accessed | tf_op | source)
XLA Modules:
  0.0 314.5 jit_solution(11281015285634961976)
XLA Ops:
  10.5 4.1 %collective-permute-start = (bf16[2,128,128]{2,1,0:T(8,128)(2,1)S(1)}, bf16[2,128,128]{2,1,0:T(8,128)(2,1)S(1)}, u32[]{:S(2)}, u32[]{:S(2)}) collective-permute-start(bf16[2,128,128]{2,1,0:T(8,128)(2,1)S(1)} %get-tuple-element.71), channel_id=1, source_target_pairs={{0,16},{2,18},{4,20},{6,22},{8,24},{10,26},{12,28},{14,30},{16,0},... | collective-permute-start | bytes 196616 | tf_op jit(solution)/shard_map/ppermute | solution.py:52
  14.6 2.4 convolution_add_fusion.3
  22.0 2.9 collective-permute-done.1
  30.0 2.5 collective-permute-done.2
  34.2 9.7 %collective-permute-done.3 = bf16[2,1024,128]{2,1,0:T(8,128)(2,1)S(1)} collective-permute-done((bf16[2,1024,128]{2,1,0:T(8,128)(2,1)S(1)}, bf16[2,1024,128]{2,1,0:T(8,128)(2,1)S(1)}, u32[]{:S(2)}, u32[]{:S(2)}) %collective-permute-start.3) | collective-permute-done | bytes 524320 | tf_op jit(solution)/shard_map/ppermute | solution.py:52
  44.0 9.6 %shard_map.272 = (f32[256,448]{1,0:T(8,128)S(1)}, bf16[256,448]{1,0:T(8,128)(2,1)S(1)}, f32[4,1,448]{2,1,0:T(1,128)S(1)}) custom-call(s32[32]{0:T(128)S(1)} %select_reduce_fusion.slot_ref, s32[4]{0:T(128)S(1)} %and_select_fusion.1.low_ref, s32[4]{0:T(128)S(1)} %fusion.43.high_ref, bf16[256,448]{1,0:T(8,128)(2,1)S(1)} %copy.135.q_ref, ...), custom_call_target="tpu_custom_call" | custom-call | flops 939524096 | bytes 4000000 | tf_op jit(solution)/shard_map/pallas_call | solution.py:246
  58.5 3.9 %fusion.55 = f32[256,2432]{1,0:T(8,128)S(1)} fusion(bf16[256,896]{1,0:T(8,128)(2,1)} %param.30, bf16[2432,896]{1,0:T(8,128)(2,1)} %param.29), kind=kOutput, calls=%fused_computation.192 | convolution fusion | flops 1115684864 | bytes 7307264 | tf_op jit(solution)/shard_map/dot_general | solution.py:402
  64.1 3.9 %fusion.54 = f32[256,2432]{1,0:T(8,128)S(1)} fusion(bf16[256,896]{1,0:T(8,128)(2,1)S(1)} %multiply_convert_fusion.3, bf16[896,2432]{1,0:T(8,128)(2,1)} %param.28), kind=kOutput, calls=%fused_computation.191 | convolution fusion | flops 1115684864 | bytes 7307264 | tf_op jit(solution)/shard_map/dot_general | solution.py:394
  86.1 4.4 %collective-permute-start.7 = (bf16[2,224,2432]{2,1,0:T(8,128)(2,1)}, bf16[2,224,2432]{2,1,0:T(8,128)(2,1)}, u32[]{:S(2)}, u32[]{:S(2)}) collective-permute-start(bf16[2,224,2432]{2,1,0:T(8,128)(2,1)} %dynamic-slice_bitcast_fusion.2), channel_id=1, source_target_pairs={{0,8},{2,10},{4,12},{6,14},{8,0},{10,2},{12,4},{14,6},{16,24},{18,... | collective-permute-start | bytes 6537224 | tf_op jit(solution)/shard_map/ppermute | solution.py:52
  94.8 10.5 %shard_map.273 = (bf16[256,448]{1,0:T(8,128)(2,1)S(1)}, bf16[2,32,64,128]{3,2,1,0:T(8,128)(2,1)S(1)}) custom-call(s32[32]{0:T(128)S(1)} %select_reduce_fusion.slot_ref, s32[4]{0:T(128)S(1)} %and_select_fusion.1.low_ref, s32[4]{0:T(128)S(1)} %fusion.43.high_ref, s32[32]{0:T(128)S(1)} %eq.40.block_ref, bf16[256,448]{1,0:T(8,128)(2,1)S(1)} %copy.135.q_ref, ...), custom_call_target="tpu_custom_call" | custom-call | flops 2348810240 | bytes 8000000 | tf_op jit(solution)/shard_map/pallas_call | solution.py:267
  112.4 5.2 %reshape.530 = bf16[4,2,112,448]{2,1,0,3:T(2,128)(2,1)S(1)} reshape(bf16[896,448]{0,1:T(8,128)(2,1)} %convolution_convert_fusion.4) | data formatting | bytes 1605632 | tf_op jit(solution)/shard_map/reshape | solution.py:77
  117.6 3.1 constant_dynamic-slice_fusion.2
  120.8 3.5 %copy.152 = bf16[4,1,112,448]{3,2,0,1:T(8,128)(2,1)} copy(bf16[4,1,112,448]{2,1,0,3:T(2,128)(2,1)} %get-tuple-element.78) | data formatting | bytes 802816
  125.2 3.4 %copy.151 = bf16[4,1,112,448]{3,2,0,1:T(8,128)(2,1)} copy(bf16[4,1,112,448]{2,1,0,3:T(2,128)(2,1)} %get-tuple-element.77) | data formatting | bytes 802816
  128.6 14.4 %collective-permute-done.16 = bf16[8,56,448]{2,1,0:T(8,128)(2,1)} collective-permute-done((bf16[8,56,448]{2,1,0:T(8,128)(2,1)}, bf16[8,56,448]{2,1,0:T(8,128)(2,1)}, u32[]{:S(2)}, u32[]{:S(2)}) %collective-permute-start.16) | collective-permute-done | bytes 401440 | tf_op jit(solution)/shard_map/ppermute | solution.py:52
  148.8 7.9 %collective-permute-done.11 = bf16[2,1024,128]{2,1,0:T(8,128)(2,1)S(1)} collective-permute-done((bf16[2,1024,128]{2,1,0:T(8,128)(2,1)}, bf16[2,1024,128]{2,1,0:T(8,128)(2,1)S(1)}, u32[]{:S(2)}, u32[]{:S(2)}) %collective-permute-start.11) | collective-permute-done | bytes 524320 | tf_op jit(solution)/shard_map/ppermute | solution.py:52
  156.9 2.9 fusion
  159.9 2.8 fusion.1
  162.7 2.1 fusion.2
  169.3 4.8 %collective-permute-done.18 = bf16[2,512,128]{2,1,0:T(8,128)(2,1)S(1)} collective-permute-done((bf16[2,512,128]{2,1,0:T(8,128)(2,1)S(1)}, bf16[2,512,128]{2,1,0:T(8,128)(2,1)S(1)}, u32[]{:S(2)}, u32[]{:S(2)}) %collective-permute-start.18) | collective-permute-done | bytes 262176 | tf_op jit(solution)/shard_map/ppermute | solution.py:52
  174.3 5.4 %collective-permute-start.19 = (bf16[2,256,128]{2,1,0:T(8,128)(2,1)S(1)}, bf16[2,256,128]{2,1,0:T(8,128)(2,1)S(1)}, u32[]{:S(2)}, u32[]{:S(2)}) collective-permute-start(bf16[2,256,128]{2,1,0:T(8,128)(2,1)S(1)} %slice.109), channel_id=1, source_target_pairs={{0,8},{2,10},{4,12},{6,14},{8,0},{10,2},{12,4},{14,6},{16,24},{18,... | collective-permute-start | bytes 393224 | tf_op jit(solution)/shard_map/ppermute | solution.py:52
  183.7 3.3 %collective-permute-start.20 = (bf16[2,128,128]{2,1,0:T(8,128)(2,1)S(1)}, bf16[2,128,128]{2,1,0:T(8,128)(2,1)S(1)}, u32[]{:S(2)}, u32[]{:S(2)}) collective-permute-start(bf16[2,128,128]{2,1,0:T(8,128)(2,1)S(1)} %slice.111), channel_id=1, source_target_pairs={{0,16},{2,18},{4,20},{6,22},{8,24},{10,26},{12,28},{14,30},{16,0},... | collective-permute-start | bytes 196616 | tf_op jit(solution)/shard_map/ppermute | solution.py:52
  187.0 40.4 %collective-permute-done.20 = bf16[2,128,128]{2,1,0:T(8,128)(2,1)S(1)} collective-permute-done((bf16[2,128,128]{2,1,0:T(8,128)(2,1)S(1)}, bf16[2,128,128]{2,1,0:T(8,128)(2,1)S(1)}, u32[]{:S(2)}, u32[]{:S(2)}) %collective-permute-start.20) | collective-permute-done | bytes 65568 | tf_op jit(solution)/shard_map/ppermute | solution.py:52
  248.5 12.1 %collective-permute-done.22 = f32[8,384]{1,0:T(8,128)S(1)} collective-permute-done((f32[8,384]{1,0:T(8,128)S(1)}, f32[8,384]{1,0:T(8,128)S(1)}, u32[]{:S(2)}, u32[]{:S(2)}) %collective-permute-start.22) | collective-permute-done | bytes 12320 | tf_op jit(solution)/shard_map/ppermute | solution.py:52
  261.3 3.0 collective-permute-done.23
  264.3 3.7 %collective-permute-done.24 = f32[8,384]{1,0:T(8,128)S(1)} collective-permute-done((f32[8,384]{1,0:T(8,128)S(1)}, f32[8,384]{1,0:T(8,128)S(1)}, u32[]{:S(2)}, u32[]{:S(2)}) %collective-permute-start.24) | collective-permute-done | bytes 12320 | tf_op jit(solution)/shard_map/ppermute | solution.py:52
  270.2 2.3 collective-permute-done.25
  282.6 2.8 collective-permute-start.36
  285.4 4.9 %collective-permute-done.34 = bf16[2,56,128]{2,1,0:T(8,128)(2,1)S(1)} collective-permute-done((bf16[2,56,128]{2,1,0:T(8,128)(2,1)S(1)}, bf16[2,56,128]{2,1,0:T(8,128)(2,1)S(1)}, u32[]{:S(2)}, u32[]{:S(2)}) %collective-permute-start.34) | collective-permute-done | bytes 28704 | tf_op jit(solution)/shard_map/ppermute | solution.py:52
  290.4 2.7 collective-permute-start.35
  293.1 12.4 %collective-permute-done.35 = bf16[1,56,128]{2,1,0:T(8,128)(2,1)S(1)} collective-permute-done((bf16[1,56,128]{2,1,0:T(8,128)(2,1)S(1)}, bf16[1,56,128]{2,1,0:T(8,128)(2,1)S(1)}, u32[]{:S(2)}, u32[]{:S(2)}) %collective-permute-start.35) | collective-permute-done | bytes 14368 | tf_op jit(solution)/shard_map/ppermute | solution.py:52
  306.9 4.4 %collective-permute-done.33 = bf16[1,56,448]{2,1,0:T(8,128)(2,1)S(1)} collective-permute-done((bf16[1,56,448]{2,1,0:T(8,128)(2,1)S(1)}, bf16[1,56,448]{2,1,0:T(8,128)(2,1)S(1)}, u32[]{:S(2)}, u32[]{:S(2)}) %collective-permute-start.33) | collective-permute-done | bytes 50208 | tf_op jit(solution)/shard_map/ppermute | solution.py:52
  (297 shorter events, 111.2 us)
Async XLA Ops:
  10.5 9.2 %collective-permute-start = (bf16[2,128,128]{2,1,0:T(8,128)(2,1)S(1)}, bf16[2,128,128]{2,1,0:T(8,128)(2,1)S(1)}, u32[]{:S(2)}, u32[]{:S(2)}) collective-permute-start(bf16[2,128,128]{2,1,0:T(8,128)(2,1)S(1)} %get-tuple-element.71), channel_id=1, source_target_pairs={{0,16},{2,18},{4,20},{6,22},{8,24},{10,26},{12,28},{14,30},{16,0},... | collective-permute-start | bytes 196616 | tf_op jit(solution)/shard_map/ppermute | solution.py:52
  32.5 11.4 %collective-permute-start.3 = (bf16[2,1024,128]{2,1,0:T(8,128)(2,1)S(1)}, bf16[2,1024,128]{2,1,0:T(8,128)(2,1)S(1)}, u32[]{:S(2)}, u32[]{:S(2)}) collective-permute-start(bf16[2,1024,128]{2,1,0:T(8,128)(2,1)S(1)} %pad_maximum_fusion), channel_id=1, source_target_pairs={{0,2},{2,0},{4,6},{6,4},{8,10},{10,8},{12,14},{14,12},{16,18},{18,... | collective-permute-start | bytes 1572872 | tf_op jit(solution)/shard_map/ppermute | solution.py:52
  79.3 11.2 %collective-permute-start.6 = (bf16[256,896]{1,0:T(8,128)(2,1)S(1)}, bf16[256,896]{1,0:T(8,128)(2,1)S(1)}, u32[]{:S(2)}, u32[]{:S(2)}) collective-permute-start(bf16[256,896]{1,0:T(8,128)(2,1)S(1)} %fusion.8), channel_id=1, source_target_pairs={{0,1},{1,0},{2,3},{3,2},{4,5},{5,4},{6,7},{7,6},{8,9},{9,8},{10,11... | collective-permute-start | bytes 1376264 | tf_op jit(solution)/shard_map/ppermute | solution.py:52
  79.9 11.1 %collective-permute-start.5 = (bf16[256,896]{1,0:T(8,128)(2,1)S(1)}, bf16[256,896]{1,0:T(8,128)(2,1)S(1)}, u32[]{:S(2)}, u32[]{:S(2)}) collective-permute-start(bf16[256,896]{1,0:T(8,128)(2,1)S(1)} %convolution_convert_fusion.5), channel_id=1, source_target_pairs={{0,1},{1,0},{2,3},{3,2},{4,5},{5,4},{6,7},{7,6},{8,9},{9,8},{10,11... | collective-permute-start | bytes 1376264 | tf_op jit(solution)/shard_map/ppermute | solution.py:52
  81.6 75.4 %collective-permute-start.9 = (bf16[4,112,2432]{2,1,0:T(8,128)(2,1)}, bf16[4,112,2432]{2,1,0:T(8,128)(2,1)}, u32[]{:S(2)}, u32[]{:S(2)}) collective-permute-start(bf16[4,112,2432]{2,1,0:T(8,128)(2,1)} %dynamic-slice_bitcast_fusion), channel_id=1, source_target_pairs={{0,4},{2,6},{4,0},{6,2},{8,12},{10,14},{12,8},{14,10},{16,20},{18,... | collective-permute-start | bytes 6537224 | tf_op jit(solution)/shard_map/ppermute | solution.py:52
  83.1 76.8 %collective-permute-start.8 = (bf16[8,56,2432]{2,1,0:T(8,128)(2,1)}, bf16[8,56,2432]{2,1,0:T(8,128)(2,1)}, u32[]{:S(2)}, u32[]{:S(2)}) collective-permute-start(bf16[8,56,2432]{2,1,0:T(8,128)(2,1)} %dynamic-slice_bitcast_fusion.1), channel_id=1, source_target_pairs={{0,2},{2,0},{4,6},{6,4},{8,10},{10,8},{12,14},{14,12},{16,18},{18,... | collective-permute-start | bytes 6537224 | tf_op jit(solution)/shard_map/ppermute | solution.py:52
  86.1 76.5 %collective-permute-start.7 = (bf16[2,224,2432]{2,1,0:T(8,128)(2,1)}, bf16[2,224,2432]{2,1,0:T(8,128)(2,1)}, u32[]{:S(2)}, u32[]{:S(2)}) collective-permute-start(bf16[2,224,2432]{2,1,0:T(8,128)(2,1)} %dynamic-slice_bitcast_fusion.2), channel_id=1, source_target_pairs={{0,8},{2,10},{4,12},{6,14},{8,0},{10,2},{12,4},{14,6},{16,24},{18,... | collective-permute-start | bytes 6537224 | tf_op jit(solution)/shard_map/ppermute | solution.py:52
  109.1 33.9 %collective-permute-start.16 = (bf16[8,56,448]{2,1,0:T(8,128)(2,1)}, bf16[8,56,448]{2,1,0:T(8,128)(2,1)}, u32[]{:S(2)}, u32[]{:S(2)}) collective-permute-start(bf16[8,56,448]{2,1,0:T(8,128)(2,1)} %dynamic-slice_bitcast_fusion.9), channel_id=1, source_target_pairs={{0,2},{2,0},{4,6},{6,4},{8,10},{10,8},{12,14},{14,12},{16,18},{18,... | collective-permute-start | bytes 1204232 | tf_op jit(solution)/shard_map/ppermute | solution.py:52
  124.3 21.4 %collective-permute-start.10 = (bf16[4,112,448]{2,1,0:T(8,128)(2,1)}, bf16[4,112,448]{2,1,0:T(8,128)(2,1)}, u32[]{:S(2)}, u32[]{:S(2)}) collective-permute-start(bf16[4,112,448]{2,1,0:T(8,128)(2,1)} %bitcast.290), channel_id=1, source_target_pairs={{0,4},{2,6},{4,0},{6,2},{8,12},{10,14},{12,8},{14,10},{16,20},{18,... | collective-permute-start | bytes 1204232 | tf_op jit(solution)/shard_map/ppermute | solution.py:52
  143.0 13.7 %collective-permute-start.11 = (bf16[2,1024,128]{2,1,0:T(8,128)(2,1)}, bf16[2,1024,128]{2,1,0:T(8,128)(2,1)S(1)}, u32[]{:S(2)}, u32[]{:S(2)}) collective-permute-start(bf16[2,1024,128]{2,1,0:T(8,128)(2,1)} %slice.107), channel_id=1, source_target_pairs={{0,2},{2,0},{4,6},{6,4},{8,10},{10,8},{12,14},{14,12},{16,18},{18,... | collective-permute-start | bytes 1572872 | tf_op jit(solution)/shard_map/ppermute | solution.py:52
  145.7 11.1 %collective-permute-start.17 = (bf16[4,56,448]{2,1,0:T(8,128)(2,1)S(1)}, bf16[4,56,448]{2,1,0:T(8,128)(2,1)S(1)}, u32[]{:S(2)}, u32[]{:S(2)}) collective-permute-start(bf16[4,56,448]{2,1,0:T(8,128)(2,1)S(1)} %dynamic-slice_bitcast_fusion.13), channel_id=1, source_target_pairs={{0,4},{2,6},{4,0},{6,2},{8,12},{10,14},{12,8},{14,10},{16,20},{18,... | collective-permute-start | bytes 602120 | tf_op jit(solution)/shard_map/ppermute | solution.py:52
  164.8 9.3 %collective-permute-start.18 = (bf16[2,512,128]{2,1,0:T(8,128)(2,1)S(1)}, bf16[2,512,128]{2,1,0:T(8,128)(2,1)S(1)}, u32[]{:S(2)}, u32[]{:S(2)}) collective-permute-start(bf16[2,512,128]{2,1,0:T(8,128)(2,1)S(1)} %slice.84), channel_id=1, source_target_pairs={{0,4},{2,6},{4,0},{6,2},{8,12},{10,14},{12,8},{14,10},{16,20},{18,... | collective-permute-start | bytes 786440 | tf_op jit(solution)/shard_map/ppermute | solution.py:52
  166.4 20.6 %collective-permute-start.15 = (bf16[4,56,448]{2,1,0:T(8,128)(2,1)S(1)}, bf16[4,56,448]{2,1,0:T(8,128)(2,1)S(1)}, u32[]{:S(2)}, u32[]{:S(2)}) collective-permute-start(bf16[4,56,448]{2,1,0:T(8,128)(2,1)S(1)} %dynamic-slice_bitcast_fusion.14), channel_id=1, source_target_pairs={{0,2},{2,0},{4,6},{6,4},{8,10},{10,8},{12,14},{14,12},{16,18},{18,... | collective-permute-start | bytes 602120 | tf_op jit(solution)/shard_map/ppermute | solution.py:52
  168.0 61.6 %collective-permute-start.14 = (bf16[4,56,2432]{2,1,0:T(8,128)(2,1)S(1)}, bf16[4,56,2432]{2,1,0:T(8,128)(2,1)S(1)}, u32[]{:S(2)}, u32[]{:S(2)}) collective-permute-start(bf16[4,56,2432]{2,1,0:T(8,128)(2,1)S(1)} %dynamic-slice_bitcast_fusion.3), channel_id=1, source_target_pairs={{0,2},{2,0},{4,6},{6,4},{8,10},{10,8},{12,14},{14,12},{16,18},{18,... | collective-permute-start | bytes 3268616 | tf_op jit(solution)/shard_map/ppermute | solution.py:52
  168.7 62.2 %collective-permute-start.13 = (bf16[4,56,2432]{2,1,0:T(8,128)(2,1)S(1)}, bf16[4,56,2432]{2,1,0:T(8,128)(2,1)S(1)}, u32[]{:S(2)}, u32[]{:S(2)}) collective-permute-start(bf16[4,56,2432]{2,1,0:T(8,128)(2,1)S(1)} %dynamic-slice_bitcast_fusion.4), channel_id=1, source_target_pairs={{0,4},{2,6},{4,0},{6,2},{8,12},{10,14},{12,8},{14,10},{16,20},{18,... | collective-permute-start | bytes 3268616 | tf_op jit(solution)/shard_map/ppermute | solution.py:52
  174.3 9.3 %collective-permute-start.19 = (bf16[2,256,128]{2,1,0:T(8,128)(2,1)S(1)}, bf16[2,256,128]{2,1,0:T(8,128)(2,1)S(1)}, u32[]{:S(2)}, u32[]{:S(2)}) collective-permute-start(bf16[2,256,128]{2,1,0:T(8,128)(2,1)S(1)} %slice.109), channel_id=1, source_target_pairs={{0,8},{2,10},{4,12},{6,14},{8,0},{10,2},{12,4},{14,6},{16,24},{18,... | collective-permute-start | bytes 393224 | tf_op jit(solution)/shard_map/ppermute | solution.py:52
  179.7 52.5 %collective-permute-start.12 = (bf16[1,224,2432]{2,1,0:T(8,128)(2,1)S(1)}, bf16[1,224,2432]{2,1,0:T(8,128)(2,1)S(1)}, u32[]{:S(2)}, u32[]{:S(2)}) collective-permute-start(bf16[1,224,2432]{2,1,0:T(8,128)(2,1)S(1)} %dynamic-slice_bitcast_fusion.5), channel_id=1, source_target_pairs={{0,16},{2,18},{4,20},{6,22},{8,24},{10,26},{12,28},{14,30},{16,0},... | collective-permute-start | bytes 3268616 | tf_op jit(solution)/shard_map/ppermute | solution.py:52
  183.7 43.7 %collective-permute-start.20 = (bf16[2,128,128]{2,1,0:T(8,128)(2,1)S(1)}, bf16[2,128,128]{2,1,0:T(8,128)(2,1)S(1)}, u32[]{:S(2)}, u32[]{:S(2)}) collective-permute-start(bf16[2,128,128]{2,1,0:T(8,128)(2,1)S(1)} %slice.111), channel_id=1, source_target_pairs={{0,16},{2,18},{4,20},{6,22},{8,24},{10,26},{12,28},{14,30},{16,0},... | collective-permute-start | bytes 196616 | tf_op jit(solution)/shard_map/ppermute | solution.py:52
  233.7 10.3 %collective-permute-start.31 = (bf16[4,112,128]{2,1,0:T(8,128)(2,1)S(1)}, bf16[4,112,128]{2,1,0:T(8,128)(2,1)S(1)}, u32[]{:S(2)}, u32[]{:S(2)}) collective-permute-start(bf16[4,112,128]{2,1,0:T(8,128)(2,1)S(1)} %dynamic-slice_bitcast_fusion.15), channel_id=1, source_target_pairs={{0,4},{2,6},{4,0},{6,2},{8,12},{10,14},{12,8},{14,10},{16,20},{18,... | collective-permute-start | bytes 344072 | tf_op jit(solution)/shard_map/ppermute | solution.py:52
  235.1 8.8 %collective-permute-start.30 = (bf16[2,56,448]{2,1,0:T(8,128)(2,1)S(1)}, bf16[2,56,448]{2,1,0:T(8,128)(2,1)S(1)}, u32[]{:S(2)}, u32[]{:S(2)}) collective-permute-start(bf16[2,56,448]{2,1,0:T(8,128)(2,1)S(1)} %dynamic-slice_bitcast_fusion.16), channel_id=1, source_target_pairs={{0,8},{2,10},{4,12},{6,14},{8,0},{10,2},{12,4},{14,6},{16,24},{18,... | collective-permute-start | bytes 301064 | tf_op jit(solution)/shard_map/ppermute | solution.py:52
  235.2 11.8 %collective-permute-start.29 = (bf16[2,56,448]{2,1,0:T(8,128)(2,1)S(1)}, bf16[2,56,448]{2,1,0:T(8,128)(2,1)S(1)}, u32[]{:S(2)}, u32[]{:S(2)}) collective-permute-start(bf16[2,56,448]{2,1,0:T(8,128)(2,1)S(1)} %dynamic-slice_bitcast_fusion.17), channel_id=1, source_target_pairs={{0,8},{2,10},{4,12},{6,14},{8,0},{10,2},{12,4},{14,6},{16,24},{18,... | collective-permute-start | bytes 301064 | tf_op jit(solution)/shard_map/ppermute | solution.py:52
  239.2 35.1 %collective-permute-start.28 = (bf16[2,56,2432]{2,1,0:T(8,128)(2,1)}, bf16[2,56,2432]{2,1,0:T(8,128)(2,1)}, u32[]{:S(2)}, u32[]{:S(2)}) collective-permute-start(bf16[2,56,2432]{2,1,0:T(8,128)(2,1)} %dynamic-slice_bitcast_fusion.6), channel_id=1, source_target_pairs={{0,8},{2,10},{4,12},{6,14},{8,0},{10,2},{12,4},{14,6},{16,24},{18,... | collective-permute-start | bytes 1634312 | tf_op jit(solution)/shard_map/ppermute | solution.py:52
  241.1 34.6 %collective-permute-start.27 = (bf16[2,56,2432]{2,1,0:T(8,128)(2,1)}, bf16[2,56,2432]{2,1,0:T(8,128)(2,1)}, u32[]{:S(2)}, u32[]{:S(2)}) collective-permute-start(bf16[2,56,2432]{2,1,0:T(8,128)(2,1)} %dynamic-slice_bitcast_fusion.7), channel_id=1, source_target_pairs={{0,8},{2,10},{4,12},{6,14},{8,0},{10,2},{12,4},{14,6},{16,24},{18,... | collective-permute-start | bytes 1634312 | tf_op jit(solution)/shard_map/ppermute | solution.py:52
  244.0 33.0 %collective-permute-start.26 = (bf16[2,56,2432]{2,1,0:T(8,128)(2,1)}, bf16[2,56,2432]{2,1,0:T(8,128)(2,1)}, u32[]{:S(2)}, u32[]{:S(2)}) collective-permute-start(bf16[2,56,2432]{2,1,0:T(8,128)(2,1)} %dynamic-slice_bitcast_fusion.8), channel_id=1, source_target_pairs={{0,2},{2,0},{4,6},{6,4},{8,10},{10,8},{12,14},{14,12},{16,18},{18,... | collective-permute-start | bytes 1634312 | tf_op jit(solution)/shard_map/ppermute | solution.py:52
  245.8 15.5 %collective-permute-start.32 = (bf16[4,56,128]{2,1,0:T(8,128)(2,1)S(1)}, bf16[4,56,128]{2,1,0:T(8,128)(2,1)S(1)}, u32[]{:S(2)}, u32[]{:S(2)}) collective-permute-start(bf16[4,56,128]{2,1,0:T(8,128)(2,1)S(1)} %dynamic-slice_bitcast_fusion.20), channel_id=1, source_target_pairs={{0,2},{2,0},{4,6},{6,4},{8,10},{10,8},{12,14},{14,12},{16,18},{18,... | collective-permute-start | bytes 172040 | tf_op jit(solution)/shard_map/ppermute | solution.py:52
  247.0 13.5 %collective-permute-start.22 = (f32[8,384]{1,0:T(8,128)S(1)}, f32[8,384]{1,0:T(8,128)S(1)}, u32[]{:S(2)}, u32[]{:S(2)}) collective-permute-start(f32[8,384]{1,0:T(8,128)S(1)} %reshape.538), channel_id=1, source_target_pairs={{0,2},{2,0},{4,6},{6,4},{8,10},{10,8},{12,14},{14,12},{16,18},{18,... | collective-permute-start | bytes 36872 | tf_op jit(solution)/shard_map/ppermute | solution.py:52
  278.3 33.7 %collective-permute-start.39 = (bf16[1,56,2432]{2,1,0:T(8,128)(2,1)S(1)}, bf16[1,56,2432]{2,1,0:T(8,128)(2,1)S(1)}, u32[]{:S(2)}, u32[]{:S(2)}) collective-permute-start(bf16[1,56,2432]{2,1,0:T(8,128)(2,1)S(1)} %dynamic-slice_bitcast_fusion.10), channel_id=1, source_target_pairs={{0,4},{2,6},{4,0},{6,2},{8,12},{10,14},{12,8},{14,10},{16,20},{18,... | collective-permute-start | bytes 817160 | tf_op jit(solution)/shard_map/ppermute | solution.py:52
  279.1 33.7 %collective-permute-start.38 = (bf16[1,56,2432]{2,1,0:T(8,128)(2,1)S(1)}, bf16[1,56,2432]{2,1,0:T(8,128)(2,1)S(1)}, u32[]{:S(2)}, u32[]{:S(2)}) collective-permute-start(bf16[1,56,2432]{2,1,0:T(8,128)(2,1)S(1)} %dynamic-slice_bitcast_fusion.11), channel_id=1, source_target_pairs={{0,16},{2,18},{4,20},{6,22},{8,24},{10,26},{12,28},{14,30},{16,0},... | collective-permute-start | bytes 817160 | tf_op jit(solution)/shard_map/ppermute | solution.py:52
  280.4 33.2 %collective-permute-start.37 = (bf16[1,56,2432]{2,1,0:T(8,128)(2,1)S(1)}, bf16[1,56,2432]{2,1,0:T(8,128)(2,1)S(1)}, u32[]{:S(2)}, u32[]{:S(2)}) collective-permute-start(bf16[1,56,2432]{2,1,0:T(8,128)(2,1)S(1)} %dynamic-slice_bitcast_fusion.12), channel_id=1, source_target_pairs={{0,16},{2,18},{4,20},{6,22},{8,24},{10,26},{12,28},{14,30},{16,0},... | collective-permute-start | bytes 817160 | tf_op jit(solution)/shard_map/ppermute | solution.py:52
  282.1 8.2 %collective-permute-start.34 = (bf16[2,56,128]{2,1,0:T(8,128)(2,1)S(1)}, bf16[2,56,128]{2,1,0:T(8,128)(2,1)S(1)}, u32[]{:S(2)}, u32[]{:S(2)}) collective-permute-start(bf16[2,56,128]{2,1,0:T(8,128)(2,1)S(1)} %dynamic-slice_bitcast_fusion.21), channel_id=1, source_target_pairs={{0,8},{2,10},{4,12},{6,14},{8,0},{10,2},{12,4},{14,6},{16,24},{18,... | collective-permute-start | bytes 86024 | tf_op jit(solution)/shard_map/ppermute | solution.py:52
  282.6 23.7 %collective-permute-start.36 = (bf16[1,56,448]{2,1,0:T(8,128)(2,1)S(1)}, bf16[1,56,448]{2,1,0:T(8,128)(2,1)S(1)}, u32[]{:S(2)}, u32[]{:S(2)}) collective-permute-start(bf16[1,56,448]{2,1,0:T(8,128)(2,1)S(1)} %dynamic-slice_bitcast_fusion.18), channel_id=1, source_target_pairs={{0,16},{2,18},{4,20},{6,22},{8,24},{10,26},{12,28},{14,30},{16,0},... | collective-permute-start | bytes 150536 | tf_op jit(solution)/shard_map/ppermute | solution.py:52
  290.4 15.1 %collective-permute-start.35 = (bf16[1,56,128]{2,1,0:T(8,128)(2,1)S(1)}, bf16[1,56,128]{2,1,0:T(8,128)(2,1)S(1)}, u32[]{:S(2)}, u32[]{:S(2)}) collective-permute-start(bf16[1,56,128]{2,1,0:T(8,128)(2,1)S(1)} %constant_dynamic-slice_fusion), channel_id=1, source_target_pairs={{0,16},{2,18},{4,20},{6,22},{8,24},{10,26},{12,28},{14,30},{16,0},... | collective-permute-start | bytes 43016 | tf_op jit(solution)/shard_map/ppermute | solution.py:52
  (45 other events, 547.9 us)

commit v2 on v1

--- a/solution.py
+++ b/solution.py
@@ -418,7 +418,7 @@
         jnp.bfloat16
     )
     other = [bits[1], bits[0]] + bits[2:]
-    last = bits[2:] + bits[:2]
+    last = bits[2:3] + bits[:2] + bits[3:]
     flow_down = RowScatter(grad_w_down, last)
     flow_gate = RowScatter(grad_w_gate, bits)
     flow_up = RowScatter(grad_w_up, other)
@@ -434,16 +434,11 @@
             jnp.float32
         )
         cur = total if bit == bits[-1] else total.astype(jnp.bfloat16)
-        if bit == bits[0]:
-            (cur,) = in_step(flows, cur)
-            for flow in flows:
-                flow.stage()
     grad_keys_own = cur[:, :, :head_dim]
     grad_values_own = cur[:, :, head_dim:]
     flow_query = RowScatter(
         jnp.dot(normed.T, grad_query_low, preferred_element_type=jnp.float32), bits
     )
-    flow_query.stage()
     flow_query.stage()
     grad_key_low = (
         rotate(grad_keys_own.reshape(seq_count, half_rows, 1, head_dim), cos_table, -sin_table)
@@ -474,7 +469,6 @@
     grad_normed = sum_pair(first_low)
     grad_in_part, grad_attn_gain = norm_back(grad_normed, x_float, inv_one, gain_one)
     grad_tokens = grad_stream + grad_in_part
-    in_step(flows + [flow_pair])
     sum_down = flow_down.finish().T
     sum_gate = flow_gate.finish()
     sum_up = flow_up.finish()

time: 315 us -> 330 us (1.048); the launches traced: 315 us -> 326 us
  waiting for transfers between devices: 128 us -> 141 us
  starting transfers between devices: 55.6 us -> 50.9 us
    ppermute x40, waiting for transfers between devices: 128 us -> 141 us  [swap(): return lax.ppermute(values, axis_name, [(i, i ^ bit) for i in range(size)])]
    ppermute x40, starting transfers between devices: 55.6 us -> 50.9 us  [swap(): return lax.ppermute(values, axis_name, [(i, i ^ bit) for i in range(size)])]
    unnamed x80 -> x92, local copies, waits for them, and re-layouts: 10.1 us -> 9.63 us
  transfers between devices with their start and end apart: 40 -> 40, of which waited for: 16 -> 23; matrix products, arithmetic and copies ran while one was open for 23% -> 24% of each run, Pallas kernels for 3% -> 3%
where the time goes in v2:
time: 330 us; the launch traced here: 326 us
  waiting for transfers between devices  141 us (43%)
  starting transfers between devices  50.9 us (15%)
  local copies, waits for them, and re-layouts  43.1 us (13%)
  other arithmetic  38.5 us (12%)
  matrix products  30.1 us (9%)
  Pallas kernels  20.4 us (6%)
    ppermute x40, waiting for transfers between devices, swap(): return lax.ppermute(values, axis_name, [(i, i ^ bit) for i in range(size)])  141 us
    ppermute x40, starting transfers between devices, swap(): return lax.ppermute(values, axis_name, [(i, i ^ bit) for i in range(size)])  50.9 us
    convert_element_type x18, other arithmetic, stage(): self.cur = total.astype(jnp.bfloat16) if self.order else total  18.4 us
    squeeze x23, local copies, waits for them, and re-layouts, stage(): send = lax.dynamic_index_in_dim(shaped, 1 - mine, 1, keepdims=False)  12.3 us
    pallas_call x1, Pallas kernels, backward(): pl.pallas_call(functools.partial(backward_kernel, key_len, head_dim ** (-...  10.5 us
    pallas_call x1, Pallas kernels, forward(): pl.pallas_call(functools.partial(forward_kernel, key_len), grid_spec=pltp...  9.93 us
    unnamed x92, local copies, waits for them, and re-layouts  9.63 us
  transfers between devices with their start and end apart: 40, of which 23 were waited for; matrix products, arithmetic and copies ran while one was open for 24% of the time, Pallas kernels for 3%

profile of v2, /device:TPU:0, one launch (start us, length us, event | category | flops | bytes accessed | tf_op | source)
XLA Modules:
  0.0 325.9 jit_solution(3096364123835273449)
XLA Ops:
  9.9 4.1 %collective-permute-start = (bf16[2,128,128]{2,1,0:T(8,128)(2,1)S(1)}, bf16[2,128,128]{2,1,0:T(8,128)(2,1)S(1)}, u32[]{:S(2)}, u32[]{:S(2)}) collective-permute-start(bf16[2,128,128]{2,1,0:T(8,128)(2,1)S(1)} %get-tuple-element.49), channel_id=1, source_target_pairs={{0,16},{2,18},{4,20},{6,22},{8,24},{10,26},{12,28},{14,30},{16,0},... | collective-permute-start | bytes 196616 | tf_op jit(solution)/shard_map/ppermute | solution.py:52
  15.1 2.4 convolution_add_fusion.3
  21.4 2.9 collective-permute-done.1
  28.8 3.0 collective-permute-done.2
  33.6 9.7 %collective-permute-done.3 = bf16[2,1024,128]{2,1,0:T(8,128)(2,1)S(1)} collective-permute-done((bf16[2,1024,128]{2,1,0:T(8,128)(2,1)S(1)}, bf16[2,1024,128]{2,1,0:T(8,128)(2,1)S(1)}, u32[]{:S(2)}, u32[]{:S(2)}) %collective-permute-start.3) | collective-permute-done | bytes 524320 | tf_op jit(solution)/shard_map/ppermute | solution.py:52
  43.4 9.9 %shard_map.272 = (f32[256,448]{1,0:T(8,128)S(1)}, bf16[256,448]{1,0:T(8,128)(2,1)S(1)}, f32[4,1,448]{2,1,0:T(1,128)S(1)}) custom-call(s32[32]{0:T(128)S(1)} %select_reduce_fusion.slot_ref, s32[4]{0:T(128)S(1)} %and_select_fusion.1.low_ref, s32[4]{0:T(128)S(1)} %fusion.37.high_ref, bf16[256,448]{1,0:T(8,128)(2,1)S(1)} %copy.127.q_ref, ...), custom_call_target="tpu_custom_call" | custom-call | flops 939524096 | bytes 4000000 | tf_op jit(solution)/shard_map/pallas_call | solution.py:246
  58.9 3.9 %fusion.49 = f32[256,2432]{1,0:T(8,128)S(1)} fusion(bf16[256,896]{1,0:T(8,128)(2,1)} %param.30, bf16[2432,896]{1,0:T(8,128)(2,1)} %param.29), kind=kOutput, calls=%fused_computation.186 | convolution fusion | flops 1115684864 | bytes 7307264 | tf_op jit(solution)/shard_map/dot_general | solution.py:402
  64.5 3.9 %fusion.48 = f32[256,2432]{1,0:T(8,128)S(1)} fusion(bf16[256,896]{1,0:T(8,128)(2,1)S(1)} %multiply_convert_fusion.3, bf16[896,2432]{1,0:T(8,128)(2,1)} %param.28), kind=kOutput, calls=%fused_computation.185 | convolution fusion | flops 1115684864 | bytes 7307264 | tf_op jit(solution)/shard_map/dot_general | solution.py:394
  84.9 2.8 collective-permute-start.8
  93.7 10.5 %shard_map.273 = (bf16[256,448]{1,0:T(8,128)(2,1)S(1)}, bf16[2,32,64,128]{3,2,1,0:T(8,128)(2,1)S(1)}) custom-call(s32[32]{0:T(128)S(1)} %select_reduce_fusion.slot_ref, s32[4]{0:T(128)S(1)} %and_select_fusion.1.low_ref, s32[4]{0:T(128)S(1)} %fusion.37.high_ref, s32[32]{0:T(128)S(1)} %eq.40.block_ref, bf16[256,448]{1,0:T(8,128)(2,1)S(1)} %copy.127.q_ref, ...), custom_call_target="tpu_custom_call" | custom-call | flops 2348810240 | bytes 8000000 | tf_op jit(solution)/shard_map/pallas_call | solution.py:267
  104.2 4.7 %collective-permute-start.12 = (bf16[2,1024,128]{2,1,0:T(8,128)(2,1)S(1)}, bf16[2,1024,128]{2,1,0:T(8,128)(2,1)}, u32[]{:S(2)}, u32[]{:S(2)}) collective-permute-start(bf16[2,1024,128]{2,1,0:T(8,128)(2,1)S(1)} %slice.107), channel_id=1, source_target_pairs={{0,2},{2,0},{4,6},{6,4},{8,10},{10,8},{12,14},{14,12},{16,18},{18,... | collective-permute-start | bytes 1572872 | tf_op jit(solution)/shard_map/ppermute | solution.py:52
  110.3 5.2 %reshape.488 = bf16[4,2,112,448]{2,1,0,3:T(2,128)(2,1)S(1)} reshape(bf16[896,448]{0,1:T(8,128)(2,1)} %convolution_convert_fusion.4) | data formatting | bytes 1605632 | tf_op jit(solution)/shard_map/reshape | solution.py:77
  116.9 30.3 %collective-permute-done.12 = bf16[2,1024,128]{2,1,0:T(8,128)(2,1)} collective-permute-done((bf16[2,1024,128]{2,1,0:T(8,128)(2,1)S(1)}, bf16[2,1024,128]{2,1,0:T(8,128)(2,1)}, u32[]{:S(2)}, u32[]{:S(2)}) %collective-permute-start.12) | collective-permute-done | bytes 524320 | tf_op jit(solution)/shard_map/ppermute | solution.py:52
  150.9 3.1 constant_dynamic-slice_fusion.7
  155.5 3.4 %copy.142 = bf16[4,1,112,448]{3,2,0,1:T(8,128)(2,1)} copy(bf16[4,1,112,448]{2,1,0,3:T(2,128)(2,1)} %get-tuple-element.56) | data formatting | bytes 802816
  160.1 2.4 copy.141
  166.0 5.1 %collective-permute-done.10 = bf16[4,112,448]{2,1,0:T(8,128)(2,1)} collective-permute-done((bf16[4,112,448]{2,1,0:T(8,128)(2,1)}, bf16[4,112,448]{2,1,0:T(8,128)(2,1)}, u32[]{:S(2)}, u32[]{:S(2)}) %collective-permute-start.10) | collective-permute-done | bytes 401440 | tf_op jit(solution)/shard_map/ppermute | solution.py:52
  177.7 3.7 %collective-permute-done.15 = bf16[2,128,128]{2,1,0:T(8,128)(2,1)S(1)} collective-permute-done((bf16[2,128,128]{2,1,0:T(8,128)(2,1)S(1)}, bf16[2,128,128]{2,1,0:T(8,128)(2,1)S(1)}, u32[]{:S(2)}, u32[]{:S(2)}) %collective-permute-start.15) | collective-permute-done | bytes 65568 | tf_op jit(solution)/shard_map/ppermute | solution.py:52
  183.7 4.3 %fusion = bf16[4,112,2432]{2,1,0:T(8,128)(2,1)} fusion(bf16[4,112,2432]{2,1,0:T(8,128)(2,1)} %collective-permute-done.9, bf16[4,2,112,2432]{3,2,1,0:T(8,128)(2,1)} %bitcast.201, s32[]{:T(128)S(6)} %select_n.206), kind=kLoop, calls=%fused_computation.5 | loop fusion | flops 4358144 | bytes 6537220 | tf_op jit(solution)/shard_map/convert_element_type | solution.py:84
  188.0 3.5 %fusion.1 = bf16[8,56,2432]{2,1,0:T(8,128)(2,1)} fusion(bf16[8,56,2432]{2,1,0:T(8,128)(2,1)} %collective-permute-done.8, bf16[8,2,56,2432]{3,2,1,0:T(8,128)(2,1)S(1)} %bitcast.199, s32[]{:T(128)S(6)} %select_n.202), kind=kLoop, calls=%fused_computation.7 | loop fusion | flops 4358144 | bytes 6537220 | tf_op jit(solution)/shard_map/convert_element_type | solution.py:84
  191.5 3.5 %fusion.2 = bf16[2,224,2432]{2,1,0:T(8,128)(2,1)} fusion(bf16[2,224,2432]{2,1,0:T(8,128)(2,1)} %collective-permute-done.7, bf16[2,2,224,2432]{3,2,1,0:T(8,128)(2,1)S(1)} %bitcast.195, s32[]{:T(128)S(6)} %select_n.199), kind=kLoop, calls=%fused_computation.9 | loop fusion | flops 4358144 | bytes 6537220 | tf_op jit(solution)/shard_map/convert_element_type | solution.py:84
  200.2 2.5 dynamic-slice_bitcast_fusion.5
  214.3 2.6 collective-permute-done.27
  218.7 4.0 %collective-permute-done.29 = bf16[2,56,448]{2,1,0:T(8,128)(2,1)S(1)} collective-permute-done((bf16[2,56,448]{2,1,0:T(8,128)(2,1)S(1)}, bf16[2,56,448]{2,1,0:T(8,128)(2,1)S(1)}, u32[]{:S(2)}, u32[]{:S(2)}) %collective-permute-start.29) | collective-permute-done | bytes 100384 | tf_op jit(solution)/shard_map/ppermute | solution.py:52
  223.8 4.3 %collective-permute-done.22 = bf16[2,56,448]{2,1,0:T(8,128)(2,1)S(1)} collective-permute-done((bf16[2,56,448]{2,1,0:T(8,128)(2,1)S(1)}, bf16[2,56,448]{2,1,0:T(8,128)(2,1)S(1)}, u32[]{:S(2)}, u32[]{:S(2)}) %collective-permute-start.22) | collective-permute-done | bytes 100384 | tf_op jit(solution)/shard_map/ppermute | solution.py:52
  233.2 2.6 collective-permute-start.17
  236.4 21.4 %collective-permute-done.17 = f32[8,384]{1,0:T(8,128)S(1)} collective-permute-done((f32[8,384]{1,0:T(8,128)S(1)}, f32[8,384]{1,0:T(8,128)S(1)}, u32[]{:S(2)}, u32[]{:S(2)}) %collective-permute-start.17) | collective-permute-done | bytes 12320 | tf_op jit(solution)/shard_map/ppermute | solution.py:52
  259.0 2.5 collective-permute-done.18
  279.6 3.8 %collective-permute-done.38 = bf16[2,56,2432]{2,1,0:T(8,128)(2,1)S(1)} collective-permute-done((bf16[2,56,2432]{2,1,0:T(8,128)(2,1)S(1)}, bf16[2,56,2432]{2,1,0:T(8,128)(2,1)S(1)}, u32[]{:S(2)}, u32[]{:S(2)}) %collective-permute-start.38) | collective-permute-done | bytes 544800 | tf_op jit(solution)/shard_map/ppermute | solution.py:52
  285.1 14.9 %collective-permute-done.35 = bf16[2,56,2432]{2,1,0:T(8,128)(2,1)S(1)} collective-permute-done((bf16[2,56,2432]{2,1,0:T(8,128)(2,1)S(1)}, bf16[2,56,2432]{2,1,0:T(8,128)(2,1)S(1)}, u32[]{:S(2)}, u32[]{:S(2)}) %collective-permute-start.35) | collective-permute-done | bytes 544800 | tf_op jit(solution)/shard_map/ppermute | solution.py:52
  300.6 5.8 %collective-permute-done.32 = bf16[2,56,2432]{2,1,0:T(8,128)(2,1)S(1)} collective-permute-done((bf16[2,56,2432]{2,1,0:T(8,128)(2,1)S(1)}, bf16[2,56,2432]{2,1,0:T(8,128)(2,1)S(1)}, u32[]{:S(2)}, u32[]{:S(2)}) %collective-permute-start.32) | collective-permute-done | bytes 544800 | tf_op jit(solution)/shard_map/ppermute | solution.py:52
  308.8 13.1 %collective-permute-done.36 = bf16[1,56,2432]{2,1,0:T(8,128)(2,1)S(1)} collective-permute-done((bf16[1,56,2432]{2,1,0:T(8,128)(2,1)S(1)}, bf16[1,56,2432]{2,1,0:T(8,128)(2,1)S(1)}, u32[]{:S(2)}, u32[]{:S(2)}) %collective-permute-start.36) | collective-permute-done | bytes 272416 | tf_op jit(solution)/shard_map/ppermute | solution.py:52
  (310 shorter events, 124.0 us)
Async XLA Ops:
  9.9 9.2 %collective-permute-start = (bf16[2,128,128]{2,1,0:T(8,128)(2,1)S(1)}, bf16[2,128,128]{2,1,0:T(8,128)(2,1)S(1)}, u32[]{:S(2)}, u32[]{:S(2)}) collective-permute-start(bf16[2,128,128]{2,1,0:T(8,128)(2,1)S(1)} %get-tuple-element.49), channel_id=1, source_target_pairs={{0,16},{2,18},{4,20},{6,22},{8,24},{10,26},{12,28},{14,30},{16,0},... | collective-permute-start | bytes 196616 | tf_op jit(solution)/shard_map/ppermute | solution.py:52
  25.1 6.8 %collective-permute-start.2 = (bf16[2,512,128]{2,1,0:T(8,128)(2,1)}, bf16[2,512,128]{2,1,0:T(8,128)(2,1)S(1)}, u32[]{:S(2)}, u32[]{:S(2)}) collective-permute-start(bf16[2,512,128]{2,1,0:T(8,128)(2,1)} %pad_maximum_fusion.1), channel_id=1, source_target_pairs={{0,4},{2,6},{4,0},{6,2},{8,12},{10,14},{12,8},{14,10},{16,20},{18,... | collective-permute-start | bytes 786440 | tf_op jit(solution)/shard_map/ppermute | solution.py:52
  32.0 11.4 %collective-permute-start.3 = (bf16[2,1024,128]{2,1,0:T(8,128)(2,1)S(1)}, bf16[2,1024,128]{2,1,0:T(8,128)(2,1)S(1)}, u32[]{:S(2)}, u32[]{:S(2)}) collective-permute-start(bf16[2,1024,128]{2,1,0:T(8,128)(2,1)S(1)} %pad_maximum_fusion), channel_id=1, source_target_pairs={{0,2},{2,0},{4,6},{6,4},{8,10},{10,8},{12,14},{14,12},{16,18},{18,... | collective-permute-start | bytes 1572872 | tf_op jit(solution)/shard_map/ppermute | solution.py:52
  54.6 8.2 %collective-permute-start.4 = (bf16[256,896]{1,0:T(8,128)(2,1)}, bf16[256,896]{1,0:T(8,128)(2,1)}, u32[]{:S(2)}, u32[]{:S(2)}) collective-permute-start(bf16[256,896]{1,0:T(8,128)(2,1)} %convolution_convert_fusion.6), channel_id=1, source_target_pairs={{0,1},{1,0},{2,3},{3,2},{4,5},{5,4},{6,7},{7,6},{8,9},{9,8},{10,11... | collective-permute-start | bytes 1376264 | tf_op jit(solution)/shard_map/ppermute | solution.py:52
  76.5 13.4 %collective-permute-start.5 = (bf16[256,896]{1,0:T(8,128)(2,1)S(1)}, bf16[256,896]{1,0:T(8,128)(2,1)S(1)}, u32[]{:S(2)}, u32[]{:S(2)}) collective-permute-start(bf16[256,896]{1,0:T(8,128)(2,1)S(1)} %convolution_convert_fusion.5), channel_id=1, source_target_pairs={{0,1},{1,0},{2,3},{3,2},{4,5},{5,4},{6,7},{7,6},{8,9},{9,8},{10,11... | collective-permute-start | bytes 1376264 | tf_op jit(solution)/shard_map/ppermute | solution.py:52
  80.2 9.2 %collective-permute-start.6 = (bf16[256,896]{1,0:T(8,128)(2,1)S(1)}, bf16[256,896]{1,0:T(8,128)(2,1)S(1)}, u32[]{:S(2)}, u32[]{:S(2)}) collective-permute-start(bf16[256,896]{1,0:T(8,128)(2,1)S(1)} %fusion.8), channel_id=1, source_target_pairs={{0,1},{1,0},{2,3},{3,2},{4,5},{5,4},{6,7},{7,6},{8,9},{9,8},{10,11... | collective-permute-start | bytes 1376264 | tf_op jit(solution)/shard_map/ppermute | solution.py:52
  81.8 101.8 %collective-permute-start.9 = (bf16[4,112,2432]{2,1,0:T(8,128)(2,1)}, bf16[4,112,2432]{2,1,0:T(8,128)(2,1)}, u32[]{:S(2)}, u32[]{:S(2)}) collective-permute-start(bf16[4,112,2432]{2,1,0:T(8,128)(2,1)} %dynamic-slice_bitcast_fusion), channel_id=1, source_target_pairs={{0,4},{2,6},{4,0},{6,2},{8,12},{10,14},{12,8},{14,10},{16,20},{18,... | collective-permute-start | bytes 6537224 | tf_op jit(solution)/shard_map/ppermute | solution.py:52
  84.9 103.1 %collective-permute-start.8 = (bf16[8,56,2432]{2,1,0:T(8,128)(2,1)}, bf16[8,56,2432]{2,1,0:T(8,128)(2,1)}, u32[]{:S(2)}, u32[]{:S(2)}) collective-permute-start(bf16[8,56,2432]{2,1,0:T(8,128)(2,1)} %dynamic-slice_bitcast_fusion.1), channel_id=1, source_target_pairs={{0,2},{2,0},{4,6},{6,4},{8,10},{10,8},{12,14},{14,12},{16,18},{18,... | collective-permute-start | bytes 6537224 | tf_op jit(solution)/shard_map/ppermute | solution.py:52
  89.1 102.4 %collective-permute-start.7 = (bf16[2,224,2432]{2,1,0:T(8,128)(2,1)}, bf16[2,224,2432]{2,1,0:T(8,128)(2,1)}, u32[]{:S(2)}, u32[]{:S(2)}) collective-permute-start(bf16[2,224,2432]{2,1,0:T(8,128)(2,1)} %dynamic-slice_bitcast_fusion.2), channel_id=1, source_target_pairs={{0,8},{2,10},{4,12},{6,14},{8,0},{10,2},{12,4},{14,6},{16,24},{18,... | collective-permute-start | bytes 6537224 | tf_op jit(solution)/shard_map/ppermute | solution.py:52
  104.2 43.0 %collective-permute-start.12 = (bf16[2,1024,128]{2,1,0:T(8,128)(2,1)S(1)}, bf16[2,1024,128]{2,1,0:T(8,128)(2,1)}, u32[]{:S(2)}, u32[]{:S(2)}) collective-permute-start(bf16[2,1024,128]{2,1,0:T(8,128)(2,1)S(1)} %slice.107), channel_id=1, source_target_pairs={{0,2},{2,0},{4,6},{6,4},{8,10},{10,8},{12,14},{14,12},{16,18},{18,... | collective-permute-start | bytes 1572872 | tf_op jit(solution)/shard_map/ppermute | solution.py:52
  149.1 13.4 %collective-permute-start.13 = (bf16[2,512,128]{2,1,0:T(8,128)(2,1)}, bf16[2,512,128]{2,1,0:T(8,128)(2,1)S(1)}, u32[]{:S(2)}, u32[]{:S(2)}) collective-permute-start(bf16[2,512,128]{2,1,0:T(8,128)(2,1)} %slice.109), channel_id=1, source_target_pairs={{0,4},{2,6},{4,0},{6,2},{8,12},{10,14},{12,8},{14,10},{16,20},{18,... | collective-permute-start | bytes 786440 | tf_op jit(solution)/shard_map/ppermute | solution.py:52
  159.0 12.2 %collective-permute-start.10 = (bf16[4,112,448]{2,1,0:T(8,128)(2,1)}, bf16[4,112,448]{2,1,0:T(8,128)(2,1)}, u32[]{:S(2)}, u32[]{:S(2)}) collective-permute-start(bf16[4,112,448]{2,1,0:T(8,128)(2,1)} %bitcast.237), channel_id=1, source_target_pairs={{0,4},{2,6},{4,0},{6,2},{8,12},{10,14},{12,8},{14,10},{16,20},{18,... | collective-permute-start | bytes 1204232 | tf_op jit(solution)/shard_map/ppermute | solution.py:52
  163.2 14.4 %collective-permute-start.11 = (bf16[8,56,448]{2,1,0:T(8,128)(2,1)}, bf16[8,56,448]{2,1,0:T(8,128)(2,1)S(1)}, u32[]{:S(2)}, u32[]{:S(2)}) collective-permute-start(bf16[8,56,448]{2,1,0:T(8,128)(2,1)} %dynamic-slice_bitcast_fusion.9), channel_id=1, source_target_pairs={{0,2},{2,0},{4,6},{6,4},{8,10},{10,8},{12,14},{14,12},{16,18},{18,... | collective-permute-start | bytes 1204232 | tf_op jit(solution)/shard_map/ppermute | solution.py:52
  176.2 5.2 %collective-permute-start.15 = (bf16[2,128,128]{2,1,0:T(8,128)(2,1)S(1)}, bf16[2,128,128]{2,1,0:T(8,128)(2,1)S(1)}, u32[]{:S(2)}, u32[]{:S(2)}) collective-permute-start(bf16[2,128,128]{2,1,0:T(8,128)(2,1)S(1)} %slice.113), channel_id=1, source_target_pairs={{0,16},{2,18},{4,20},{6,22},{8,24},{10,26},{12,28},{14,30},{16,0},... | collective-permute-start | bytes 196616 | tf_op jit(solution)/shard_map/ppermute | solution.py:52
  195.9 6.8 %collective-permute-start.24 = (bf16[4,112,128]{2,1,0:T(8,128)(2,1)S(1)}, bf16[4,112,128]{2,1,0:T(8,128)(2,1)S(1)}, u32[]{:S(2)}, u32[]{:S(2)}) collective-permute-start(bf16[4,112,128]{2,1,0:T(8,128)(2,1)S(1)} %dynamic-slice_bitcast_fusion.13), channel_id=1, source_target_pairs={{0,4},{2,6},{4,0},{6,2},{8,12},{10,14},{12,8},{14,10},{16,20},{18,... | collective-permute-start | bytes 344072 | tf_op jit(solution)/shard_map/ppermute | solution.py:52
  196.5 15.0 %collective-permute-start.28 = (bf16[4,56,448]{2,1,0:T(8,128)(2,1)S(1)}, bf16[4,56,448]{2,1,0:T(8,128)(2,1)S(1)}, u32[]{:S(2)}, u32[]{:S(2)}) collective-permute-start(bf16[4,56,448]{2,1,0:T(8,128)(2,1)S(1)} %dynamic-slice_bitcast_fusion.10), channel_id=1, source_target_pairs={{0,2},{2,0},{4,6},{6,4},{8,10},{10,8},{12,14},{14,12},{16,18},{18,... | collective-permute-start | bytes 602120 | tf_op jit(solution)/shard_map/ppermute | solution.py:52
  198.7 13.5 %collective-permute-start.21 = (bf16[4,56,448]{2,1,0:T(8,128)(2,1)}, bf16[4,56,448]{2,1,0:T(8,128)(2,1)S(1)}, u32[]{:S(2)}, u32[]{:S(2)}) collective-permute-start(bf16[4,56,448]{2,1,0:T(8,128)(2,1)} %dynamic-slice_bitcast_fusion.11), channel_id=1, source_target_pairs={{0,4},{2,6},{4,0},{6,2},{8,12},{10,14},{12,8},{14,10},{16,20},{18,... | collective-permute-start | bytes 602120 | tf_op jit(solution)/shard_map/ppermute | solution.py:52
  200.2 29.8 %collective-permute-start.16 = (bf16[256,896]{1,0:T(8,128)(2,1)S(1)}, bf16[256,896]{1,0:T(8,128)(2,1)S(1)}, u32[]{:S(2)}, u32[]{:S(2)}) collective-permute-start(bf16[256,896]{1,0:T(8,128)(2,1)S(1)} %fusion.7), channel_id=1, source_target_pairs={{0,1},{1,0},{2,3},{3,2},{4,5},{5,4},{6,7},{7,6},{8,9},{9,8},{10,11... | collective-permute-start | bytes 1376264 | tf_op jit(solution)/shard_map/ppermute | solution.py:52
  208.4 63.2 %collective-permute-start.37 = (bf16[4,56,2432]{2,1,0:T(8,128)(2,1)}, bf16[4,56,2432]{2,1,0:T(8,128)(2,1)}, u32[]{:S(2)}, u32[]{:S(2)}) collective-permute-start(bf16[4,56,2432]{2,1,0:T(8,128)(2,1)} %dynamic-slice_bitcast_fusion.3), channel_id=1, source_target_pairs={{0,2},{2,0},{4,6},{6,4},{8,10},{10,8},{12,14},{14,12},{16,18},{18,... | collective-permute-start | bytes 3268616 | tf_op jit(solution)/shard_map/ppermute | solution.py:52
  211.1 63.1 %collective-permute-start.34 = (bf16[4,56,2432]{2,1,0:T(8,128)(2,1)}, bf16[4,56,2432]{2,1,0:T(8,128)(2,1)}, u32[]{:S(2)}, u32[]{:S(2)}) collective-permute-start(bf16[4,56,2432]{2,1,0:T(8,128)(2,1)} %dynamic-slice_bitcast_fusion.4), channel_id=1, source_target_pairs={{0,2},{2,0},{4,6},{6,4},{8,10},{10,8},{12,14},{14,12},{16,18},{18,... | collective-permute-start | bytes 3268616 | tf_op jit(solution)/shard_map/ppermute | solution.py:52
  211.4 66.2 %collective-permute-start.31 = (bf16[4,56,2432]{2,1,0:T(8,128)(2,1)}, bf16[4,56,2432]{2,1,0:T(8,128)(2,1)}, u32[]{:S(2)}, u32[]{:S(2)}) collective-permute-start(bf16[4,56,2432]{2,1,0:T(8,128)(2,1)} %dynamic-slice_bitcast_fusion.5), channel_id=1, source_target_pairs={{0,4},{2,6},{4,0},{6,2},{8,12},{10,14},{12,8},{14,10},{16,20},{18,... | collective-permute-start | bytes 3268616 | tf_op jit(solution)/shard_map/ppermute | solution.py:52
  216.9 5.8 %collective-permute-start.29 = (bf16[2,56,448]{2,1,0:T(8,128)(2,1)S(1)}, bf16[2,56,448]{2,1,0:T(8,128)(2,1)S(1)}, u32[]{:S(2)}, u32[]{:S(2)}) collective-permute-start(bf16[2,56,448]{2,1,0:T(8,128)(2,1)S(1)} %dynamic-slice_bitcast_fusion.12), channel_id=1, source_target_pairs={{0,8},{2,10},{4,12},{6,14},{8,0},{10,2},{12,4},{14,6},{16,24},{18,... | collective-permute-start | bytes 301064 | tf_op jit(solution)/shard_map/ppermute | solution.py:52
  222.7 5.4 %collective-permute-start.22 = (bf16[2,56,448]{2,1,0:T(8,128)(2,1)S(1)}, bf16[2,56,448]{2,1,0:T(8,128)(2,1)S(1)}, u32[]{:S(2)}, u32[]{:S(2)}) collective-permute-start(bf16[2,56,448]{2,1,0:T(8,128)(2,1)S(1)} %dynamic-slice_bitcast_fusion.14), channel_id=1, source_target_pairs={{0,8},{2,10},{4,12},{6,14},{8,0},{10,2},{12,4},{14,6},{16,24},{18,... | collective-permute-start | bytes 301064 | tf_op jit(solution)/shard_map/ppermute | solution.py:52
  228.1 5.1 %collective-permute-start.30 = (bf16[1,56,448]{2,1,0:T(8,128)(2,1)S(1)}, bf16[1,56,448]{2,1,0:T(8,128)(2,1)S(1)}, u32[]{:S(2)}, u32[]{:S(2)}) collective-permute-start(bf16[1,56,448]{2,1,0:T(8,128)(2,1)S(1)} %constant_dynamic-slice_fusion.3), channel_id=1, source_target_pairs={{0,16},{2,18},{4,20},{6,22},{8,24},{10,26},{12,28},{14,30},{16,0},... | collective-permute-start | bytes 150536 | tf_op jit(solution)/shard_map/ppermute | solution.py:52
  230.0 28.3 %collective-permute-start.23 = (bf16[1,56,448]{2,1,0:T(8,128)(2,1)S(1)}, bf16[1,56,448]{2,1,0:T(8,128)(2,1)S(1)}, u32[]{:S(2)}, u32[]{:S(2)}) collective-permute-start(bf16[1,56,448]{2,1,0:T(8,128)(2,1)S(1)} %constant_dynamic-slice_fusion.5), channel_id=1, source_target_pairs={{0,16},{2,18},{4,20},{6,22},{8,24},{10,26},{12,28},{14,30},{16,0},... | collective-permute-start | bytes 150536 | tf_op jit(solution)/shard_map/ppermute | solution.py:52
  233.2 24.6 %collective-permute-start.17 = (f32[8,384]{1,0:T(8,128)S(1)}, f32[8,384]{1,0:T(8,128)S(1)}, u32[]{:S(2)}, u32[]{:S(2)}) collective-permute-start(f32[8,384]{1,0:T(8,128)S(1)} %reshape.492), channel_id=1, source_target_pairs={{0,2},{2,0},{4,6},{6,4},{8,10},{10,8},{12,14},{14,12},{16,18},{18,... | collective-permute-start | bytes 36872 | tf_op jit(solution)/shard_map/ppermute | solution.py:52
  273.6 9.7 %collective-permute-start.38 = (bf16[2,56,2432]{2,1,0:T(8,128)(2,1)S(1)}, bf16[2,56,2432]{2,1,0:T(8,128)(2,1)S(1)}, u32[]{:S(2)}, u32[]{:S(2)}) collective-permute-start(bf16[2,56,2432]{2,1,0:T(8,128)(2,1)S(1)} %dynamic-slice_bitcast_fusion.6), channel_id=1, source_target_pairs={{0,4},{2,6},{4,0},{6,2},{8,12},{10,14},{12,8},{14,10},{16,20},{18,... | collective-permute-start | bytes 1634312 | tf_op jit(solution)/shard_map/ppermute | solution.py:52
  275.9 24.1 %collective-permute-start.35 = (bf16[2,56,2432]{2,1,0:T(8,128)(2,1)S(1)}, bf16[2,56,2432]{2,1,0:T(8,128)(2,1)S(1)}, u32[]{:S(2)}, u32[]{:S(2)}) collective-permute-start(bf16[2,56,2432]{2,1,0:T(8,128)(2,1)S(1)} %dynamic-slice_bitcast_fusion.7), channel_id=1, source_target_pairs={{0,8},{2,10},{4,12},{6,14},{8,0},{10,2},{12,4},{14,6},{16,24},{18,... | collective-permute-start | bytes 1634312 | tf_op jit(solution)/shard_map/ppermute | solution.py:52
  279.3 27.2 %collective-permute-start.32 = (bf16[2,56,2432]{2,1,0:T(8,128)(2,1)S(1)}, bf16[2,56,2432]{2,1,0:T(8,128)(2,1)S(1)}, u32[]{:S(2)}, u32[]{:S(2)}) collective-permute-start(bf16[2,56,2432]{2,1,0:T(8,128)(2,1)S(1)} %dynamic-slice_bitcast_fusion.8), channel_id=1, source_target_pairs={{0,8},{2,10},{4,12},{6,14},{8,0},{10,2},{12,4},{14,6},{16,24},{18,... | collective-permute-start | bytes 1634312 | tf_op jit(solution)/shard_map/ppermute | solution.py:52
  283.5 24.4 %collective-permute-start.39 = (bf16[1,56,2432]{2,1,0:T(8,128)(2,1)S(1)}, bf16[1,56,2432]{2,1,0:T(8,128)(2,1)S(1)}, u32[]{:S(2)}, u32[]{:S(2)}) collective-permute-start(bf16[1,56,2432]{2,1,0:T(8,128)(2,1)S(1)} %constant_dynamic-slice_fusion), channel_id=1, source_target_pairs={{0,16},{2,18},{4,20},{6,22},{8,24},{10,26},{12,28},{14,30},{16,0},... | collective-permute-start | bytes 817160 | tf_op jit(solution)/shard_map/ppermute | solution.py:52
  300.2 21.7 %collective-permute-start.36 = (bf16[1,56,2432]{2,1,0:T(8,128)(2,1)S(1)}, bf16[1,56,2432]{2,1,0:T(8,128)(2,1)S(1)}, u32[]{:S(2)}, u32[]{:S(2)}) collective-permute-start(bf16[1,56,2432]{2,1,0:T(8,128)(2,1)S(1)} %constant_dynamic-slice_fusion.1), channel_id=1, source_target_pairs={{0,16},{2,18},{4,20},{6,22},{8,24},{10,26},{12,28},{14,30},{16,0},... | collective-permute-start | bytes 817160 | tf_op jit(solution)/shard_map/ppermute | solution.py:52
  306.6 18.2 %collective-permute-start.33 = (bf16[1,56,2432]{2,1,0:T(8,128)(2,1)S(1)}, bf16[1,56,2432]{2,1,0:T(8,128)(2,1)S(1)}, u32[]{:S(2)}, u32[]{:S(2)}) collective-permute-start(bf16[1,56,2432]{2,1,0:T(8,128)(2,1)S(1)} %constant_dynamic-slice_fusion.2), channel_id=1, source_target_pairs={{0,16},{2,18},{4,20},{6,22},{8,24},{10,26},{12,28},{14,30},{16,0},... | collective-permute-start | bytes 817160 | tf_op jit(solution)/shard_map/ppermute | solution.py:52
  (51 other events, 509.1 us)
